TPU v7x, 32 devices: a whole 2x2x4 slice. The times are simulated.
32 devices in a mesh: slab: 4 (over y, core), tile: 8 (over z, x).
Axes of the slice: x: 2, y: 2, z: 4, core: 2. Of those that a mesh axis runs over, the one named last changes fastest.
Arguments:
- particles: float32 [8, 65536], P(None, ('slab', 'tile')), may hold values from -6 to 6, as said below
- halo_up: int32 [32], P(('slab', 'tile')), may hold values from 0 to 15
- halo_down: int32 [32], P(('slab', 'tile')), may hold values from 0 to 15
- tile_first: int32 [4, 1024], P('slab', 'tile'), may hold values from 0 to 127, as said below
- tile_second: int32 [4, 1024], P('slab', 'tile'), may hold values from 0 to 143
- tile_live: int32 [4, 1024], P('slab', 'tile'), may hold values from 0 to 1, as said below
- step_index: int32 [1], replicated, may hold values from 0 to 63
- time_step: float32 [1], replicated, may hold values from 0.05 to 0.5
Outputs:
- rates: float32 [4, 65536], P(None, ('slab', 'tile'))
- advanced: float32 [7, 65536], P(None, ('slab', 'tile'))
Inputs may be any that keep to these rules, and one draw needn't show every extreme that they name: `particles`: densities lie between 0.85 and 1.15, masses between 0.0002 and 0.0008, positions between 0 and 3. `tile_first`: in each slab the 16 blocks of each device of the slab are named by exactly 128 of the slab's slots. `tile_live`: in each slab exactly half of the 1024 slots are live; how many fall on one device varies.
All inputs are finite; a program needn't handle non-finite values.
Results may differ from a plain program's by a relative error of at most 0.00018.
Values sent between devices are 32-bit elements; how exact they have to be, the bound alone decides.
No kernel may reach another device: no remote copies, remote signals or barrier semaphores. Data moves between devices by JAX's collectives and lax.ppermute only.
A program may use at most 64 MiB of HBM per device.

v0:
```python
import functools

import jax
import jax.numpy as jnp
from jax import lax
from jax.experimental import pallas as pl
from jax.experimental.pallas import tpu as pltpu
from jax.sharding import PartitionSpec as P

PB = 128
BLK_DEV = 16

SMOOTHING = 1.0
KERNEL_NORM = 21.0 / (16.0 * 3.141592653589793)
SOUND_SPEED = 10.0
STIFFNESS = SOUND_SPEED * SOUND_SPEED / 7.0
VISCOSITY = 0.1
BLAST_STRENGTH = 8.0
DECAY_TIME = 8.0

KAPPA = (5.0 * KERNEL_NORM) ** (1.0 / 3.0)
SCALE = 0.5 * KAPPA
SCALE_SQ = SCALE * SCALE
CENTRE = 1.5
DENSITY_SCALE = -0.5 / (VISCOSITY * SOUND_SPEED * SMOOTHING * SCALE_SQ)
UNROLL = 8
ROWS = 32

F32 = jnp.float32
BF16 = jnp.bfloat16
VMEM = pl.BlockSpec(memory_space=pltpu.VMEM)
SMEM = pl.BlockSpec(memory_space=pltpu.SMEM)
PARAMS = pltpu.CompilerParams(vmem_limit_bytes=48 * 1024 * 1024)


def split_3(value):
    first = value.astype(BF16).astype(F32)
    rest = value - first
    second = rest.astype(BF16).astype(F32)
    return first, second, rest - second


def stacked(parts, order):
    return [parts[k] for k in order]


def divided(value, by):
    if by & (by - 1) == 0:
        return lax.shift_right_logical(value, by.bit_length() - 1)
    return jnp.floor((value.astype(F32) + 0.5) * (1.0 / by)).astype(jnp.int32)


def pre_kernel(up_ids, down_ids, particles, first, second, live, pair_out, up_out, down_out):
    width = particles.shape[1]
    pair_out[:, 0:width] = particles[...]
    pair_out[:, width : width + PB] = jnp.zeros((8, PB), F32)
    for row, values in enumerate((first, second, live)):
        pair_out[row : row + 1, width : width + PB] = values[...].astype(F32)
    for ids, out in ((up_ids, up_out), (down_ids, down_out)):
        for item in range(out.shape[1] // PB):
            start = pl.multiple_of(ids[item] * PB, PB)
            out[:, item * PB : (item + 1) * PB] = particles[:, pl.ds(start, PB)]


def mid_kernel(pair, partner, below, above, column_out):
    width = pair.shape[1] - PB
    rim = below.shape[1]
    column_out[:, 0:width] = pair[:, 0:width]
    column_out[:, width : width + rim] = below[...]
    column_out[:, width + rim : width + 2 * rim] = above[...]
    column_out[:, width + 2 * rim :] = pair[:, width:]
    column_out[3:6, width + 2 * rim :] = partner[0:3, width:]


def pressure_term(density):
    term = STIFFNESS * (density**7 - 1.0) / (density * density)
    return jnp.where(density > 0.0, term, 0.0)


def pair_kernel(shifts, rim, *refs):
    columns = refs[:shifts]
    partner, own_out, other_out = refs[shifts : shifts + 3]
    acting, summing, receiving, sums, products, parts, lists, codes, codes_smem, sem = refs[shifts + 3 :]
    dev_blocks = BLK_DEV + 2 * rim
    tile = lax.axis_index("tile")
    row, column = lax.div(tile, 2), lax.rem(tile, 2)
    list_start = dev_blocks * PB
    holders = 2 * shifts
    slots = codes.shape[1]

    for shift in range(shifts):
        for side in range(2):
            for kind in range(3):
                lists[kind, 2 * shift + side : 2 * shift + side + 1, :] = columns[shift][
                    3 * side + kind : 3 * side + kind + 1, list_start : list_start + PB
                ]
    first = lists[0].astype(jnp.int32)
    second = lists[1].astype(jnp.int32)
    slab_blocks = holders * BLK_DEV
    is_rim = second >= slab_blocks
    rim_number = second - slab_blocks
    is_above = rim_number >= holders * rim
    rim_number = jnp.where(is_above, rim_number - holders * rim, rim_number)
    rim_owner = divided(rim_number, rim)
    owner = jnp.where(is_rim, rim_owner, divided(second, BLK_DEV))
    place = jnp.where(
        is_rim,
        BLK_DEV + rim_number - rim_owner * rim + jnp.where(is_above, rim, 0),
        second & (BLK_DEV - 1),
    )
    behind = row - divided(owner, 2)
    behind = jnp.where(behind < 0, behind + shifts, behind)
    target = divided(first, BLK_DEV)
    mine = (lists[2] > 0.5) & (divided(target, 2) == row) & ((owner & 1) == column)
    receiver = (first & (BLK_DEV - 1)) + jnp.where((target & 1) == column, 0, BLK_DEV)
    code = receiver * 1024 + behind * dev_blocks + place
    chosen = jnp.where(mine, 1.0, 0.0)
    lane = lax.broadcasted_iota(jnp.int32, (PB, PB), 1)
    sublane = lax.broadcasted_iota(jnp.int32, (PB, PB), 0)
    earlier = jnp.where(sublane < lane, 1.0, 0.0).astype(BF16)
    rank = jnp.dot(chosen.astype(BF16), earlier, preferred_element_type=F32)
    counts = jnp.sum(chosen, axis=1, keepdims=True)
    offset = jnp.zeros((1, 1), F32)
    offsets = []
    for holder in range(holders):
        offsets.append(offset)
        offset = offset + counts[holder : holder + 1]
    rank = rank + jnp.concatenate(offsets, axis=0)
    count = jnp.max(offset).astype(jnp.int32)
    rank = jnp.where(mine, rank.astype(jnp.int32), -1)
    dummy = 2 * BLK_DEV * 1024
    spread = lax.broadcasted_iota(jnp.int32, (PB, slots), 1)
    rank_t = jnp.transpose(jnp.concatenate([rank, jnp.zeros((PB - holders, PB), jnp.int32)], axis=0))
    code_t = jnp.transpose(
        jnp.concatenate([code - dummy, jnp.zeros((PB - holders, PB), jnp.int32)], axis=0)
    )
    found = jnp.zeros((8, slots), jnp.int32)
    for holder in range(holders):
        placed = jnp.where(
            rank_t[:, holder : holder + 1] == spread, code_t[:, holder : holder + 1], 0
        )
        for start in range(0, PB, 8):
            found = found + placed[start : start + 8]
    codes[...] = jnp.broadcast_to(jnp.sum(found, axis=0, keepdims=True) + dummy, codes.shape)
    copy = pltpu.make_async_copy(codes, codes_smem, sem)
    copy.start()

    row_8 = lax.broadcasted_iota(jnp.int32, (8, PB), 0)
    centre = jnp.where(row_8 < 3, CENTRE, 0.0)
    scale = jnp.where(row_8 < 3, SCALE, 0.0)
    blank = jnp.zeros((8, PB), F32)

    def fields(block):
        moved = block - centre
        scaled = moved * scale
        norm = jnp.sum(scaled * scaled, axis=0, keepdims=True)
        inner = jnp.sum(moved[0:3] * moved[3:6], axis=0, keepdims=True)
        density = block[6:7]
        return moved, scaled, norm, inner, density * DENSITY_SCALE, pressure_term(density), block[7:8]

    def by_row(*rows):
        value = rows[-1]
        for row, other in zip(range(len(rows) - 2, -1, -1), rows[-2::-1]):
            value = jnp.where(row_8 == row, other, value)
        return value

    first_order, second_order = (0, 1, 0, 1, 2, 0), (0, 0, 1, 1, 0, 2)

    def columns_of(near, meet, rest, orders):
        rows = stacked(split_3(near), orders) + stacked(split_3(meet), orders)
        rows += stacked(split_3(rest), orders[:3]) + [blank]
        return jnp.concatenate(rows, axis=0).astype(BF16)

    def prepare_receiving(number, block):
        moved, scaled, norm, inner, density, pressure, mass = fields(block)
        near = jnp.where(row_8 < 3, scaled, by_row(0.0, 0.0, 0.0, norm, 1.0, 0.0))
        meet = jnp.concatenate([moved[3:6], moved[0:3], inner, jnp.ones((1, PB), F32)], axis=0)
        sparse = [
            columns_of(near, blank, blank, second_order),
            columns_of(blank, meet, blank, second_order),
            columns_of(blank, blank, by_row(density, 1.0, 0.0), second_order),
            columns_of(blank, blank, by_row(0.0, 0.0, pressure, 1.0, 0.0), second_order),
        ]
        for k in range(4):
            receiving[number, :, k * PB : (k + 1) * PB] = sparse[k]

    def prepare_acting(number, block):
        moved, scaled, norm, inner, density, pressure, mass = fields(block)
        near = jnp.where(row_8 < 3, -2.0 * scaled, by_row(0.0, 0.0, 0.0, 1.0, norm, 0.0))
        meet = jnp.where(row_8 < 6, -moved, jnp.where(row_8 == 6, 1.0, inner)) * mass
        rest = by_row(1.0, density, mass, mass * pressure, 0.0)
        acting[number] = columns_of(near, meet, rest, first_order)
        spot = split_3(jnp.where(row_8 < 3, moved, jnp.where(row_8 == 3, 1.0, 0.0)))
        summing[number, :, 0:PB] = jnp.concatenate([*spot, blank], axis=0).astype(BF16)
        summing[number, :, PB:] = jnp.concatenate([spot[0], spot[1], blank, blank], axis=0).astype(BF16)

    def block_at(ref, number):
        return ref[:, pl.ds(pl.multiple_of(number * PB, PB), PB)]

    def each_receiving(number, carry):
        prepare_receiving(number, block_at(columns[0], number))
        prepare_receiving(number + BLK_DEV, block_at(partner, number))
        return carry

    def each_acting(number, carry):
        for shift in range(shifts):
            prepare_acting(shift * dev_blocks + number, block_at(columns[shift], number))
        return carry

    lax.fori_loop(0, BLK_DEV, each_receiving, 0)
    receiving[2 * BLK_DEV] = jnp.zeros(receiving.shape[1:], BF16)
    lax.fori_loop(0, dev_blocks, each_acting, 0)
    sums[...] = jnp.zeros(sums.shape, F32)
    copy.wait()

    def work(turn, carry):
        items = [codes_smem[0, turn * UNROLL + lot] for lot in range(UNROLL)]
        targets = [lax.shift_right_logical(item, 10) for item in items]
        sources = [item & 1023 for item in items]
        for lot in range(UNROLL):
            products[lot] = lax.dot_general(
                acting[sources[lot]],
                receiving[targets[lot]],
                (((0,), (0,)), ((), ())),
                preferred_element_type=F32,
            )
        closings = []
        for lot in range(UNROLL):
            closing_sum = jnp.zeros((8, PB), F32)
            for start in range(0, PB, ROWS):
                span = slice(start, start + ROWS)
                dist_sq = jnp.maximum(products[lot, span, 0:PB], 1e-12)
                approach = products[lot, span, PB : 2 * PB]
                support = jnp.maximum(KAPPA - dist_sq * lax.rsqrt(dist_sq), 0.0)
                gradient = support * support * support
                closing = approach * gradient
                weight = (dist_sq + 0.01 * SMOOTHING * SMOOTHING * SCALE_SQ) * products[
                    lot, span, 2 * PB : 3 * PB
                ]
                damping = jnp.minimum(approach, 0.0) * pl.reciprocal(weight, approx=True)
                push = (products[lot, span, 3 * PB :] + damping) * gradient
                high = push.astype(BF16)
                parts[lot, start : start + ROWS, :] = high
                parts[lot, PB + start : PB + start + ROWS, :] = (push - high.astype(F32)).astype(BF16)
                for part in range(0, ROWS, 8):
                    closing_sum = closing_sum + closing[part : part + 8]
            closings.append(closing_sum)
        for lot in range(UNROLL):
            total = jnp.dot(summing[sources[lot]], parts[lot], preferred_element_type=F32)
            sums[targets[lot], 0:8, :] += closings[lot]
            sums[targets[lot], 8:16, :] += total[0:8] + total[8:16] + total[16:24]
        return carry

    lax.fori_loop(0, lax.div(count + UNROLL - 1, UNROLL), work, 0)

    for number in range(BLK_DEV):
        place = slice(number * PB, (number + 1) * PB)
        for base, source, out in ((0, columns[0], own_out), (BLK_DEV, partner, other_out)):
            out[0:1, place] = -jnp.sum(sums[base + number, 0:8, :], axis=0, keepdims=True)
            out[1:4, place] = (source[0:3, place] - CENTRE) * sums[base + number, 11:12, :] - sums[
                base + number, 8:11, :
            ]


def finish_kernel(step_index, time_step, particles, own, other, rates_out, advanced_out):
    step_length = time_step[0]
    elapsed = step_index[0].astype(F32) * step_length
    strength = BLAST_STRENGTH * jnp.exp(jnp.full((1, PB), -elapsed / DECAY_TIME, F32))[:, 0:1]
    block = particles[...]
    tile_rates = own[...] + other[...]
    relative = block[0:3] + 1.0
    spread_sq = jnp.sum(relative * relative, axis=0, keepdims=True) + 1.0
    source = strength * relative / (spread_sq * jnp.sqrt(spread_sq))
    forcing = tile_rates[1:4] + source
    rates_out[0:1] = tile_rates[0:1]
    rates_out[1:4] = forcing
    velocity = block[3:6] + step_length * forcing
    advanced_out[0:3] = block[0:3] + step_length * velocity
    advanced_out[3:6] = velocity
    advanced_out[6:7] = block[6:7] + step_length * tile_rates[0:1]


def pair_sums(columns, partner, rim):
    shifts, width = len(columns), partner.shape[1] - PB
    dev_blocks = BLK_DEV + 2 * rim
    receivers, actors = 2 * BLK_DEV + 1, shifts * dev_blocks
    slots = 3 * PB
    partial = jax.ShapeDtypeStruct((4, width), F32)
    return pl.pallas_call(
        functools.partial(pair_kernel, shifts, rim),
        out_shape=(partial, partial),
        in_specs=[VMEM] * (shifts + 1),
        out_specs=(VMEM, VMEM),
        scratch_shapes=[
            pltpu.VMEM((actors, PB, PB), BF16),
            pltpu.VMEM((actors, 32, 2 * PB), BF16),
            pltpu.VMEM((receivers, PB, 4 * PB), BF16),
            pltpu.VMEM((receivers, 16, PB), F32),
            pltpu.VMEM((UNROLL, PB, 4 * PB), F32),
            pltpu.VMEM((UNROLL, 2 * PB, PB), BF16),
            pltpu.VMEM((3, 2 * shifts, PB), F32),
            pltpu.VMEM((8, slots), jnp.int32),
            pltpu.SMEM((8, slots), jnp.int32),
            pltpu.SemaphoreType.DMA,
        ],
        compiler_params=PARAMS,
        name="pairs",
    )(*columns, partner)


def on_device(
    particles, halo_up, halo_down, tile_first, tile_second, tile_live, step_index, time_step
):
    width = particles.shape[1]
    rim = halo_up.shape[0]
    rim_width = rim * PB
    tiles, slabs = lax.axis_size("tile"), lax.axis_size("slab")
    shifts = tiles // 2
    pair, sent_up, sent_down = pl.pallas_call(
        pre_kernel,
        out_shape=(
            jax.ShapeDtypeStruct((8, width + PB), F32),
            jax.ShapeDtypeStruct((8, rim_width), F32),
            jax.ShapeDtypeStruct((8, rim_width), F32),
        ),
        in_specs=[SMEM, SMEM, VMEM, VMEM, VMEM, VMEM],
        out_specs=(VMEM, VMEM, VMEM),
        name="pack",
    )(halo_up, halo_down, particles, tile_first, tile_second, tile_live)
    across = [(i, i ^ 1) for i in range(tiles)]
    partner = lax.ppermute(pair, "tile", across)
    below = lax.ppermute(sent_up, "slab", [(i, i + 1) for i in range(slabs - 1)])
    above = lax.ppermute(sent_down, "slab", [(i + 1, i) for i in range(slabs - 1)])
    column = pl.pallas_call(
        mid_kernel,
        out_shape=jax.ShapeDtypeStruct((8, width + 2 * rim_width + PB), F32),
        in_specs=[VMEM] * 4,
        out_specs=VMEM,
        name="join",
    )(pair, partner, below, above)
    columns = [column]
    for shift in range(1, shifts):
        ring = [(i, (i + 2 * shift) % tiles) for i in range(tiles)]
        columns.append(lax.ppermute(column, "tile", ring))
    own, other = pair_sums(columns, partner, rim)
    other = lax.ppermute(other, "tile", across)
    return pl.pallas_call(
        finish_kernel,
        out_shape=(
            jax.ShapeDtypeStruct((4, width), F32),
            jax.ShapeDtypeStruct((7, width), F32),
        ),
        in_specs=[SMEM, SMEM, VMEM, VMEM, VMEM],
        out_specs=(VMEM, VMEM),
        name="advance",
    )(step_index, time_step, particles, own, other)


def solution(mesh):
    placed = (
        P(None, ("slab", "tile")),
        P(("slab", "tile")),
        P(("slab", "tile")),
        P("slab", "tile"),
        P("slab", "tile"),
        P("slab", "tile"),
        P(),
        P(),
    )
    return jax.shard_map(
        on_device,
        mesh=mesh,
        in_specs=placed,
        out_specs=(P(None, ("slab", "tile")), P(None, ("slab", "tile"))),
        check_vma=False,
    )
```

profile of v0, /device:TPU:0, one launch (start us, length us, event | category | flops | bytes accessed | tf_op | source)
XLA Modules:
  0.0 42.0 jit_solution(17979867414437227006)
XLA Ops:
  1.9 1.5 %pack.1 = (f32[8,2176]{1,0:T(8,128)}, f32[8,128]{1,0:T(8,128)}, f32[8,128]{1,0:T(8,128)}) custom-call(s32[1]{0:T(128)S(6)} %copy.10.up_ids, s32[1]{0:T(128)S(6)} %copy.11.down_ids, f32[8,2048]{1,0:T(8,128)} %particles.3, s32[1,128]{1,0:T(1,128)} %first.1, s32[1,128]{1,0:T(1,128)} %second.1, s32[1,128]{1,0:T(1,128)} %live.1), custom_call_target="tpu_custom_call" | custom-call | tf_op jit(solution)/shard_map/pack/pallas_call | solution.py:319
  3.4 0.0 copy-start.7
  3.4 2.9 %collective-permute-start = (f32[8,2176]{1,0:T(8,128)}, f32[8,2176]{1,0:T(8,128)S(1)}, u32[]{:S(2)}, u32[]{:S(2)}) collective-permute-start(f32[8,2176]{1,0:T(8,128)} %get-tuple-element.7.pair), channel_id=1, source_target_pairs={{0,1},{1,0},{2,3},{3,2},{4,5},{5,4},{6,7},{7,6},{8,9},{9,8},{10,11... | collective-permute-start | bytes 208904 | tf_op jit(solution)/shard_map/ppermute | solution.py:331
  6.4 1.4 %collective-permute-start.1 = (f32[8,128]{1,0:T(8,128)}, f32[8,128]{1,0:T(8,128)S(1)}, u32[]{:S(2)}, u32[]{:S(2)}) collective-permute-start(f32[8,128]{1,0:T(8,128)} %get-tuple-element.8), channel_id=1, source_target_pairs={{0,8},{8,16},{16,24},{1,9},{9,17},{17,25},{2,10},{10,18},{18,26},{... | collective-permute-start | bytes 12296 | tf_op jit(solution)/shard_map/ppermute | solution.py:332
  7.8 0.0 copy-done.7
  7.8 1.3 %collective-permute-start.2 = (f32[8,128]{1,0:T(8,128)S(1)}, f32[8,128]{1,0:T(8,128)S(1)}, u32[]{:S(2)}, u32[]{:S(2)}) collective-permute-start(f32[8,128]{1,0:T(8,128)S(1)} %copy-done.7), channel_id=1, source_target_pairs={{8,0},{16,8},{24,16},{9,1},{17,9},{25,17},{10,2},{18,10},{26,18},{... | collective-permute-start | bytes 12296 | tf_op jit(solution)/shard_map/ppermute | solution.py:333
  9.1 0.0 collective-permute-done.1.below
  9.1 0.0 copy-start.5
  9.2 3.3 %collective-permute-done.2.above = f32[8,128]{1,0:T(8,128)S(1)} collective-permute-done((f32[8,128]{1,0:T(8,128)S(1)}, f32[8,128]{1,0:T(8,128)S(1)}, u32[]{:S(2)}, u32[]{:S(2)}) %collective-permute-start.2) | collective-permute-done | bytes 4128 | tf_op jit(solution)/shard_map/ppermute | solution.py:333
  12.5 0.0 copy-start.6
  12.5 0.0 collective-permute-done.partner.refs_4_
  12.5 0.0 copy-done.5
  12.5 0.6 %copy-done.6 = f32[8,128]{1,0:T(8,128)} copy-done((f32[8,128]{1,0:T(8,128)}, f32[8,128]{1,0:T(8,128)S(1)}, u32[]{:S(2)}) %copy-start.6) | copy-done | bytes 4120
  13.1 0.0 copy-start.1
  13.1 0.6 %copy-done.1 = f32[8,2176]{1,0:T(8,128)} copy-done((f32[8,2176]{1,0:T(8,128)}, f32[8,2176]{1,0:T(8,128)S(1)}, u32[]{:S(2)}) %copy-start.1) | copy-done | bytes 69656
  13.7 1.6 %join.1.refs_0_ = f32[8,2432]{1,0:T(8,128)} custom-call(f32[8,2176]{1,0:T(8,128)} %get-tuple-element.7.pair, f32[8,2176]{1,0:T(8,128)} %copy-done.1, f32[8,128]{1,0:T(8,128)} %copy-done.5, f32[8,128]{1,0:T(8,128)} %copy-done.6), custom_call_target="tpu_custom_call" | custom-call | tf_op jit(solution)/shard_map/join/pallas_call | solution.py:334
  15.3 1.6 %collective-permute-start.3 = (f32[8,2432]{1,0:T(8,128)}, f32[8,2432]{1,0:T(8,128)S(1)}, u32[]{:S(2)}, u32[]{:S(2)}) collective-permute-start(f32[8,2432]{1,0:T(8,128)} %join.1.refs_0_), channel_id=1, source_target_pairs={{0,2},{1,3},{2,4},{3,5},{4,6},{5,7},{6,0},{7,1},{8,10},{9,11},{10,... | collective-permute-start | bytes 233480 | tf_op jit(solution)/shard_map/ppermute | solution.py:344
  16.8 2.6 %collective-permute-start.4 = (f32[8,2432]{1,0:T(8,128)}, f32[8,2432]{1,0:T(8,128)S(1)}, u32[]{:S(2)}, u32[]{:S(2)}) collective-permute-start(f32[8,2432]{1,0:T(8,128)} %join.1.refs_0_), channel_id=1, source_target_pairs={{0,4},{1,5},{2,6},{3,7},{4,0},{5,1},{6,2},{7,3},{8,12},{9,13},{10,... | collective-permute-start | bytes 233480 | tf_op jit(solution)/shard_map/ppermute | solution.py:344
  19.4 1.3 %collective-permute-start.5 = (f32[8,2432]{1,0:T(8,128)}, f32[8,2432]{1,0:T(8,128)S(1)}, u32[]{:S(2)}, u32[]{:S(2)}) collective-permute-start(f32[8,2432]{1,0:T(8,128)} %join.1.refs_0_), channel_id=1, source_target_pairs={{0,6},{1,7},{2,0},{3,1},{4,2},{5,3},{6,4},{7,5},{8,14},{9,15},{10,... | collective-permute-start | bytes 233480 | tf_op jit(solution)/shard_map/ppermute | solution.py:344
  20.8 0.9 %collective-permute-done.3.refs_1_ = f32[8,2432]{1,0:T(8,128)S(1)} collective-permute-done((f32[8,2432]{1,0:T(8,128)}, f32[8,2432]{1,0:T(8,128)S(1)}, u32[]{:S(2)}, u32[]{:S(2)}) %collective-permute-start.3) | collective-permute-done | bytes 77856 | tf_op jit(solution)/shard_map/ppermute | solution.py:344
  21.7 3.1 %collective-permute-done.4.refs_2_ = f32[8,2432]{1,0:T(8,128)S(1)} collective-permute-done((f32[8,2432]{1,0:T(8,128)}, f32[8,2432]{1,0:T(8,128)S(1)}, u32[]{:S(2)}, u32[]{:S(2)}) %collective-permute-start.4) | collective-permute-done | bytes 77856 | tf_op jit(solution)/shard_map/ppermute | solution.py:344
  24.8 0.2 collective-permute-done.5.refs_3_
  24.9 0.0 copy-start
  24.9 0.9 %copy-done = f32[8,2432]{1,0:T(8,128)S(1)} copy-done((f32[8,2432]{1,0:T(8,128)S(1)}, f32[8,2432]{1,0:T(8,128)}, u32[]{:S(2)}) %copy-start) | copy-done | bytes 77848
  25.8 0.0 copy-start.2
  25.8 0.9 %copy-done.2 = f32[8,2176]{1,0:T(8,128)S(1)} copy-done((f32[8,2176]{1,0:T(8,128)S(1)}, f32[8,2176]{1,0:T(8,128)}, u32[]{:S(2)}) %copy-start.2) | copy-done | bytes 69656
  26.7 8.6 %pairs.1 = (f32[4,2048]{1,0:T(4,128)S(1)}, f32[4,2048]{1,0:T(4,128)S(1)}) custom-call(f32[8,2432]{1,0:T(8,128)S(1)} %copy-done, f32[8,2432]{1,0:T(8,128)S(1)} %collective-permute-done.3.refs_1_, f32[8,2432]{1,0:T(8,128)S(1)} %collective-permute-done.4.refs_2_, f32[8,2432]{1,0:T(8,128)S(1)} %collective-permute-done.5.refs_3_, f32[8,2176]{1,0:T(8,128)S(1)} %copy-done.2), custom_call_target="tpu_custom_call" | custom-call | tf_op jit(solution)/shard_map/pairs/pallas_call | solution.py:289
  35.3 0.0 copy-start.3
  35.3 0.6 %copy-done.3 = f32[4,2048]{1,0:T(4,128)} copy-done((f32[4,2048]{1,0:T(4,128)}, f32[4,2048]{1,0:T(4,128)S(1)}, u32[]{:S(2)}) %copy-start.3) | copy-done | bytes 32792
  35.9 1.2 %collective-permute-start.6 = (f32[4,2048]{1,0:T(4,128)S(1)}, f32[4,2048]{1,0:T(4,128)S(1)}, u32[]{:S(2)}, u32[]{:S(2)}) collective-permute-start(f32[4,2048]{1,0:T(4,128)S(1)} %get-tuple-element.11), channel_id=1, source_target_pairs={{0,1},{1,0},{2,3},{3,2},{4,5},{5,4},{6,7},{7,6},{8,9},{9,8},{10,11... | collective-permute-start | bytes 98312 | tf_op jit(solution)/shard_map/ppermute | solution.py:346
  38.4 1.4 %collective-permute-done.6.other = f32[4,2048]{1,0:T(4,128)S(1)} collective-permute-done((f32[4,2048]{1,0:T(4,128)S(1)}, f32[4,2048]{1,0:T(4,128)S(1)}, u32[]{:S(2)}, u32[]{:S(2)}) %collective-permute-start.6) | collective-permute-done | bytes 32800 | tf_op jit(solution)/shard_map/ppermute | solution.py:346
  39.8 0.0 copy-start.4
  39.8 0.6 %copy-done.4 = f32[4,2048]{1,0:T(4,128)} copy-done((f32[4,2048]{1,0:T(4,128)}, f32[4,2048]{1,0:T(4,128)S(1)}, u32[]{:S(2)}) %copy-start.4) | copy-done | bytes 32792
  40.4 1.6 %advance.1 = (f32[4,2048]{1,0:T(4,128)}, f32[7,2048]{1,0:T(8,128)}) custom-call(s32[1]{0:T(128)S(6)} %copy.12.step_index, f32[1]{0:T(128)S(6)} %copy.13.time_step, f32[8,2048]{1,0:T(8,128)} %particles.3, f32[4,2048]{1,0:T(4,128)} %copy-done.3, f32[4,2048]{1,0:T(4,128)} %copy-done.4), custom_call_target="tpu_custom_call" | custom-call | tf_op jit(solution)/shard_map/advance/pallas_call | solution.py:347
Async XLA Ops:
  3.4 4.4 %copy-start.7 = (f32[8,128]{1,0:T(8,128)S(1)}, f32[8,128]{1,0:T(8,128)}, u32[]{:S(2)}) copy-start(f32[8,128]{1,0:T(8,128)} %get-tuple-element.9) | copy-start | bytes 12292
  3.4 9.1 %collective-permute-start = (f32[8,2176]{1,0:T(8,128)}, f32[8,2176]{1,0:T(8,128)S(1)}, u32[]{:S(2)}, u32[]{:S(2)}) collective-permute-start(f32[8,2176]{1,0:T(8,128)} %get-tuple-element.7.pair), channel_id=1, source_target_pairs={{0,1},{1,0},{2,3},{3,2},{4,5},{5,4},{6,7},{7,6},{8,9},{9,8},{10,11... | collective-permute-start | bytes 208904 | tf_op jit(solution)/shard_map/ppermute | solution.py:331
  6.4 2.8 %collective-permute-start.1 = (f32[8,128]{1,0:T(8,128)}, f32[8,128]{1,0:T(8,128)S(1)}, u32[]{:S(2)}, u32[]{:S(2)}) collective-permute-start(f32[8,128]{1,0:T(8,128)} %get-tuple-element.8), channel_id=1, source_target_pairs={{0,8},{8,16},{16,24},{1,9},{9,17},{17,25},{2,10},{10,18},{18,26},{... | collective-permute-start | bytes 12296 | tf_op jit(solution)/shard_map/ppermute | solution.py:332
  7.8 4.6 %collective-permute-start.2 = (f32[8,128]{1,0:T(8,128)S(1)}, f32[8,128]{1,0:T(8,128)S(1)}, u32[]{:S(2)}, u32[]{:S(2)}) collective-permute-start(f32[8,128]{1,0:T(8,128)S(1)} %copy-done.7), channel_id=1, source_target_pairs={{8,0},{16,8},{24,16},{9,1},{17,9},{25,17},{10,2},{18,10},{26,18},{... | collective-permute-start | bytes 12296 | tf_op jit(solution)/shard_map/ppermute | solution.py:333
  9.1 3.3 %copy-start.5 = (f32[8,128]{1,0:T(8,128)}, f32[8,128]{1,0:T(8,128)S(1)}, u32[]{:S(2)}) copy-start(f32[8,128]{1,0:T(8,128)S(1)} %collective-permute-done.1.below) | copy-start | bytes 12292
  12.5 0.6 %copy-start.6 = (f32[8,128]{1,0:T(8,128)}, f32[8,128]{1,0:T(8,128)S(1)}, u32[]{:S(2)}) copy-start(f32[8,128]{1,0:T(8,128)S(1)} %collective-permute-done.2.above) | copy-start | bytes 12292
  13.1 0.6 %copy-start.1 = (f32[8,2176]{1,0:T(8,128)}, f32[8,2176]{1,0:T(8,128)S(1)}, u32[]{:S(2)}) copy-start(f32[8,2176]{1,0:T(8,128)S(1)} %collective-permute-done.partner.refs_4_) | copy-start | bytes 208900
  15.3 6.4 %collective-permute-start.3 = (f32[8,2432]{1,0:T(8,128)}, f32[8,2432]{1,0:T(8,128)S(1)}, u32[]{:S(2)}, u32[]{:S(2)}) collective-permute-start(f32[8,2432]{1,0:T(8,128)} %join.1.refs_0_), channel_id=1, source_target_pairs={{0,2},{1,3},{2,4},{3,5},{4,6},{5,7},{6,0},{7,1},{8,10},{9,11},{10,... | collective-permute-start | bytes 233480 | tf_op jit(solution)/shard_map/ppermute | solution.py:344
  16.8 7.9 %collective-permute-start.4 = (f32[8,2432]{1,0:T(8,128)}, f32[8,2432]{1,0:T(8,128)S(1)}, u32[]{:S(2)}, u32[]{:S(2)}) collective-permute-start(f32[8,2432]{1,0:T(8,128)} %join.1.refs_0_), channel_id=1, source_target_pairs={{0,4},{1,5},{2,6},{3,7},{4,0},{5,1},{6,2},{7,3},{8,12},{9,13},{10,... | collective-permute-start | bytes 233480 | tf_op jit(solution)/shard_map/ppermute | solution.py:344
  19.4 5.5 %collective-permute-start.5 = (f32[8,2432]{1,0:T(8,128)}, f32[8,2432]{1,0:T(8,128)S(1)}, u32[]{:S(2)}, u32[]{:S(2)}) collective-permute-start(f32[8,2432]{1,0:T(8,128)} %join.1.refs_0_), channel_id=1, source_target_pairs={{0,6},{1,7},{2,0},{3,1},{4,2},{5,3},{6,4},{7,5},{8,14},{9,15},{10,... | collective-permute-start | bytes 233480 | tf_op jit(solution)/shard_map/ppermute | solution.py:344
  24.9 0.9 %copy-start = (f32[8,2432]{1,0:T(8,128)S(1)}, f32[8,2432]{1,0:T(8,128)}, u32[]{:S(2)}) copy-start(f32[8,2432]{1,0:T(8,128)} %join.1.refs_0_) | copy-start | bytes 233476
  25.8 0.9 %copy-start.2 = (f32[8,2176]{1,0:T(8,128)S(1)}, f32[8,2176]{1,0:T(8,128)}, u32[]{:S(2)}) copy-start(f32[8,2176]{1,0:T(8,128)} %copy-done.1) | copy-start | bytes 208900
  35.3 0.6 %copy-start.3 = (f32[4,2048]{1,0:T(4,128)}, f32[4,2048]{1,0:T(4,128)S(1)}, u32[]{:S(2)}) copy-start(f32[4,2048]{1,0:T(4,128)S(1)} %get-tuple-element.10.own) | copy-start | bytes 98308
  35.9 3.9 %collective-permute-start.6 = (f32[4,2048]{1,0:T(4,128)S(1)}, f32[4,2048]{1,0:T(4,128)S(1)}, u32[]{:S(2)}, u32[]{:S(2)}) collective-permute-start(f32[4,2048]{1,0:T(4,128)S(1)} %get-tuple-element.11), channel_id=1, source_target_pairs={{0,1},{1,0},{2,3},{3,2},{4,5},{5,4},{6,7},{7,6},{8,9},{9,8},{10,11... | collective-permute-start | bytes 98312 | tf_op jit(solution)/shard_map/ppermute | solution.py:346
  39.8 0.6 %copy-start.4 = (f32[4,2048]{1,0:T(4,128)}, f32[4,2048]{1,0:T(4,128)S(1)}, u32[]{:S(2)}) copy-start(f32[4,2048]{1,0:T(4,128)S(1)} %collective-permute-done.6.other) | copy-start | bytes 98308
where the time goes:
time: 42.5 us; the launch traced here: 42 us
  Pallas kernels  13.2 us (31%)
  starting transfers between devices  12.4 us (29%)
  waiting for transfers between devices  8.85 us (21%)
  local copies, waits for them, and re-layouts  4.2 us (10%)
  between operations  3.29 us (8%)
    pallas_call x1, Pallas kernels, pair_sums(): pl.pallas_call(functools.partial(pair_kernel, shifts, rim), out_shape=(pa...  8.59 us
    ppermute x3, starting transfers between devices, on_device(): columns.append(lax.ppermute(column, 'tile', ring))  5.51 us
    unnamed x16, local copies, waits for them, and re-layouts  4.2 us
    ppermute x3, waiting for transfers between devices, on_device(): columns.append(lax.ppermute(column, 'tile', ring))  4.15 us
    ppermute x1, waiting for transfers between devices, on_device(): lax.ppermute(sent_down, 'slab', [(i + 1, i) for i in range(slabs - 1)])  3.32 us
    ppermute x1, starting transfers between devices, on_device(): partner = lax.ppermute(pair, 'tile', across)  2.94 us
    pallas_call x1, Pallas kernels, on_device(): pl.pallas_call(finish_kernel, out_shape=(jax.ShapeDtypeStruct((4, width),...  1.58 us
    pallas_call x1, Pallas kernels, on_device(): pl.pallas_call(mid_kernel, out_shape=jax.ShapeDtypeStruct((8, width + 2 *...  1.56 us
  transfers between devices with their start and end apart: 7, of which 5 were waited for; matrix products, arithmetic and copies ran while one was open for 0% of the time, Pallas kernels for 0%

commit v1 on v0

--- a/solution.py
+++ b/solution.py
@@ -30,7 +30,9 @@
 BF16 = jnp.bfloat16
 VMEM = pl.BlockSpec(memory_space=pltpu.VMEM)
 SMEM = pl.BlockSpec(memory_space=pltpu.SMEM)
-PARAMS = pltpu.CompilerParams(vmem_limit_bytes=48 * 1024 * 1024)
+HBM = pl.BlockSpec(memory_space=pltpu.HBM)
+PAIRS = pltpu.CompilerParams(vmem_limit_bytes=48 * 1024 * 1024)
+SMALL = pltpu.CompilerParams(vmem_limit_bytes=4 * 1024 * 1024)
 
 
 def split_3(value):
@@ -50,24 +52,40 @@
     return jnp.floor((value.astype(F32) + 0.5) * (1.0 / by)).astype(jnp.int32)
 
 
-def pre_kernel(up_ids, down_ids, particles, first, second, live, pair_out, up_out, down_out):
+def pack_kernel(particles, first, second, live, pair_out, lists, sems):
     width = particles.shape[1]
-    pair_out[:, 0:width] = particles[...]
+    moves = [(values, lists.at[kind]) for kind, values in enumerate((first, second, live))]
+    moves.append((particles, pair_out.at[:, 0:width]))
+    copies = [pltpu.make_async_copy(*move, sems.at[k]) for k, move in enumerate(moves)]
+    for copy in copies:
+        copy.start()
+    for copy in copies:
+        copy.wait()
     pair_out[:, width : width + PB] = jnp.zeros((8, PB), F32)
-    for row, values in enumerate((first, second, live)):
-        pair_out[row : row + 1, width : width + PB] = values[...].astype(F32)
-    for ids, out in ((up_ids, up_out), (down_ids, down_out)):
-        for item in range(out.shape[1] // PB):
-            start = pl.multiple_of(ids[item] * PB, PB)
-            out[:, item * PB : (item + 1) * PB] = particles[:, pl.ds(start, PB)]
-
-
-def mid_kernel(pair, partner, below, above, column_out):
+    for kind in range(3):
+        pair_out[kind : kind + 1, width : width + PB] = lists[kind].astype(F32)
+
+
+def rim_kernel(up_ids, down_ids, pair, near_out, far_out):
+    is_odd = lax.rem(lax.axis_index("slab"), 2)
+    for item in range(up_ids.shape[0]):
+        up, down = up_ids[item], down_ids[item]
+        change = is_odd * (down - up)
+        for number, out in ((up + change, near_out), (down - change, far_out)):
+            start = pl.multiple_of(number * PB, PB)
+            out[:, item * PB : (item + 1) * PB] = pair[:, pl.ds(start, PB)]
+
+
+def join_kernel(pair, partner, near, far, column_out):
     width = pair.shape[1] - PB
-    rim = below.shape[1]
+    rim = near.shape[1]
+    slab = lax.axis_index("slab")
+    is_odd = lax.rem(slab, 2) == 1
+    below = jnp.where(is_odd, near[...], far[...])
+    above = jnp.where(is_odd, far[...], near[...])
     column_out[:, 0:width] = pair[:, 0:width]
-    column_out[:, width : width + rim] = below[...]
-    column_out[:, width + rim : width + 2 * rim] = above[...]
+    column_out[:, width : width + rim] = jnp.where(slab > 0, below, 0.0)
+    column_out[:, width + rim : width + 2 * rim] = jnp.where(slab < lax.axis_size("slab") - 1, above, 0.0)
     column_out[:, width + 2 * rim :] = pair[:, width:]
     column_out[3:6, width + 2 * rim :] = partner[0:3, width:]
 
@@ -262,10 +280,11 @@
             ]
 
 
-def finish_kernel(step_index, time_step, particles, own, other, rates_out, advanced_out):
-    step_length = time_step[0]
-    elapsed = step_index[0].astype(F32) * step_length
-    strength = BLAST_STRENGTH * jnp.exp(jnp.full((1, PB), -elapsed / DECAY_TIME, F32))[:, 0:1]
+def advance_kernel(step, particles, own, other, rates_out, advanced_out):
+    step_length = step[0:1]
+    elapsed = step[1:2] * step_length
+    strength = BLAST_STRENGTH * jnp.exp(-elapsed / DECAY_TIME)
+    step_length, strength = step_length[:, 0:1], strength[:, 0:1]
     block = particles[...]
     tile_rates = own[...] + other[...]
     relative = block[0:3] + 1.0
@@ -303,7 +322,7 @@
             pltpu.SMEM((8, slots), jnp.int32),
             pltpu.SemaphoreType.DMA,
         ],
-        compiler_params=PARAMS,
+        compiler_params=PAIRS,
         name="pairs",
     )(*columns, partner)
 
@@ -316,44 +335,61 @@
     rim_width = rim * PB
     tiles, slabs = lax.axis_size("tile"), lax.axis_size("slab")
     shifts = tiles // 2
-    pair, sent_up, sent_down = pl.pallas_call(
-        pre_kernel,
-        out_shape=(
-            jax.ShapeDtypeStruct((8, width + PB), F32),
-            jax.ShapeDtypeStruct((8, rim_width), F32),
-            jax.ShapeDtypeStruct((8, rim_width), F32),
-        ),
-        in_specs=[SMEM, SMEM, VMEM, VMEM, VMEM, VMEM],
-        out_specs=(VMEM, VMEM, VMEM),
+    given = (particles, tile_first, tile_second, tile_live)
+    given = [pltpu.with_memory_space_constraint(array, pltpu.HBM) for array in given]
+    pair = pl.pallas_call(
+        pack_kernel,
+        out_shape=jax.ShapeDtypeStruct((8, width + PB), F32),
+        in_specs=[HBM] * 4,
+        out_specs=VMEM,
+        scratch_shapes=[
+            pltpu.VMEM((3, 1, tile_first.shape[-1]), jnp.int32),
+            pltpu.SemaphoreType.DMA((4,)),
+        ],
+        compiler_params=SMALL,
         name="pack",
-    )(halo_up, halo_down, particles, tile_first, tile_second, tile_live)
+    )(*given)
     across = [(i, i ^ 1) for i in range(tiles)]
+    evens = [(i, i ^ 1) for i in range(slabs)]
+    odds = [(i, (i + 1 if i % 2 else i - 1) % slabs) for i in range(slabs)]
     partner = lax.ppermute(pair, "tile", across)
-    below = lax.ppermute(sent_up, "slab", [(i, i + 1) for i in range(slabs - 1)])
-    above = lax.ppermute(sent_down, "slab", [(i + 1, i) for i in range(slabs - 1)])
+    near, far = pl.pallas_call(
+        rim_kernel,
+        out_shape=[jax.ShapeDtypeStruct((8, rim_width), F32)] * 2,
+        in_specs=[SMEM, SMEM, VMEM],
+        out_specs=(VMEM, VMEM),
+        compiler_params=SMALL,
+        name="rim",
+    )(halo_up, halo_down, pair)
+    near = lax.ppermute(near, "slab", evens)
+    far = lax.ppermute(far, "slab", odds)
     column = pl.pallas_call(
-        mid_kernel,
+        join_kernel,
         out_shape=jax.ShapeDtypeStruct((8, width + 2 * rim_width + PB), F32),
         in_specs=[VMEM] * 4,
         out_specs=VMEM,
+        compiler_params=SMALL,
         name="join",
-    )(pair, partner, below, above)
-    columns = [column]
-    for shift in range(1, shifts):
+    )(pair, partner, near, far)
+    columns = [column] * shifts
+    for shift in sorted(range(1, shifts), key=lambda k: min(k, shifts - k)):
         ring = [(i, (i + 2 * shift) % tiles) for i in range(tiles)]
-        columns.append(lax.ppermute(column, "tile", ring))
+        columns[shift] = lax.ppermute(column, "tile", ring)
     own, other = pair_sums(columns, partner, rim)
+    step = jnp.concatenate([time_step, step_index.astype(F32)])
+    step = jnp.broadcast_to(step[:, None], (2, PB))
     other = lax.ppermute(other, "tile", across)
     return pl.pallas_call(
-        finish_kernel,
+        advance_kernel,
         out_shape=(
             jax.ShapeDtypeStruct((4, width), F32),
             jax.ShapeDtypeStruct((7, width), F32),
         ),
-        in_specs=[SMEM, SMEM, VMEM, VMEM, VMEM],
+        in_specs=[VMEM] * 4,
         out_specs=(VMEM, VMEM),
+        compiler_params=SMALL,
         name="advance",
-    )(step_index, time_step, particles, own, other)
+    )(step, particles, own, other)
 
 
 def solution(mesh):

time: 42.5 us -> 32.6 us (0.77); the launches traced: 42 us -> 32.7 us
  local copies, waits for them, and re-layouts: 4.2 us -> 0.08 us
  Pallas kernels: 13.2 us -> 10.3 us
  starting transfers between devices: 12.4 us -> 10.3 us
    unnamed x16 -> x2, local copies, waits for them, and re-layouts: 4.2 us -> 0.01 us
    pallas_call x3 -> x4, Pallas kernels: 4.65 us -> 1.69 us  [the longest x1 0.93 us: on_device(): pl.pallas_call(pack_kernel, out_shape=jax.ShapeDtypeStruct((8, width + PB...]
    ppermute x5, waiting for transfers between devices: 7.47 us -> 4.77 us  [the longest x3 3.31 us: on_device(): columns[shift] = lax.ppermute(column, 'tile', ring)]
    ppermute x1, waiting for transfers between devices: 1.37 us -> 3.82 us  [on_device(): other = lax.ppermute(other, 'tile', across)]
    ppermute x1, starting transfers between devices: 1.24 us -> 0.07 us  [on_device(): other = lax.ppermute(other, 'tile', across)]
    ppermute x5, starting transfers between devices: 8.25 us -> 7.27 us  [the longest x3 5.57 us: on_device(): columns[shift] = lax.ppermute(column, 'tile', ring)]
where the time goes in v1:
time: 32.6 us; the launch traced here: 32.7 us
  Pallas kernels  10.3 us (32%)
  starting transfers between devices  10.3 us (32%)
  waiting for transfers between devices  8.59 us (26%)
  between operations  3.29 us (10%)
    pallas_call x1, Pallas kernels, pair_sums(): pl.pallas_call(functools.partial(pair_kernel, shifts, rim), out_shape=(pa...  8.61 us
    ppermute x3, starting transfers between devices, on_device(): columns[shift] = lax.ppermute(column, 'tile', ring)  5.57 us
    ppermute x1, waiting for transfers between devices, on_device(): other = lax.ppermute(other, 'tile', across)  3.82 us
    ppermute x3, waiting for transfers between devices, on_device(): columns[shift] = lax.ppermute(column, 'tile', ring)  3.31 us
    ppermute x1, starting transfers between devices, on_device(): partner = lax.ppermute(pair, 'tile', across)  3 us
    ppermute x1, starting transfers between devices, on_device(): far = lax.ppermute(far, 'slab', odds)  1.64 us
    ppermute x1, waiting for transfers between devices, on_device(): far = lax.ppermute(far, 'slab', odds)  1.46 us
    pallas_call x1, Pallas kernels, on_device(): pl.pallas_call(pack_kernel, out_shape=jax.ShapeDtypeStruct((8, width + PB...  0.93 us
  transfers between devices with their start and end apart: 7, of which 5 were waited for; matrix products, arithmetic and copies ran while one was open for 0% of the time, Pallas kernels for 0%

profile of v1, /device:TPU:0, one launch (start us, length us, event | category | flops | bytes accessed | tf_op | source)
XLA Modules:
  0.0 32.7 jit_solution(2805560144148540974)
XLA Ops:
  0.6 0.9 %pack.1.pair = f32[8,2176]{1,0:T(8,128)S(1)} custom-call(f32[8,2048]{1,0:T(8,128)} %particles.3, s32[1,128]{1,0:T(1,128)} %first.1, s32[1,128]{1,0:T(1,128)} %second.1, s32[1,128]{1,0:T(1,128)} %live.1), custom_call_target="tpu_custom_call" | custom-call | tf_op jit(solution)/shard_map/pack/pallas_call | solution.py:340
  1.6 3.0 %collective-permute-start = (f32[8,2176]{1,0:T(8,128)S(1)}, f32[8,2176]{1,0:T(8,128)S(1)}, u32[]{:S(2)}, u32[]{:S(2)}) collective-permute-start(f32[8,2176]{1,0:T(8,128)S(1)} %pack.1.pair), channel_id=1, source_target_pairs={{0,1},{1,0},{2,3},{3,2},{4,5},{5,4},{6,7},{7,6},{8,9},{9,8},{10,11... | collective-permute-start | bytes 208904 | tf_op jit(solution)/shard_map/ppermute | solution.py:355
  5.9 0.1 collective-permute-start.1
  6.0 1.6 %collective-permute-start.2 = (f32[8,128]{1,0:T(8,128)S(1)}, f32[8,128]{1,0:T(8,128)S(1)}, u32[]{:S(2)}, u32[]{:S(2)}) collective-permute-start(f32[8,128]{1,0:T(8,128)S(1)} %get-tuple-element.7), channel_id=1, source_target_pairs={{0,24},{8,16},{16,8},{24,0},{1,25},{9,17},{17,9},{25,1},{2,26},{10... | collective-permute-start | bytes 12296 | tf_op jit(solution)/shard_map/ppermute | solution.py:365
  7.6 0.0 collective-permute-done.1.near
  7.6 1.5 %collective-permute-done.2.far = f32[8,128]{1,0:T(8,128)S(1)} collective-permute-done((f32[8,128]{1,0:T(8,128)S(1)}, f32[8,128]{1,0:T(8,128)S(1)}, u32[]{:S(2)}, u32[]{:S(2)}) %collective-permute-start.2) | collective-permute-done | bytes 4128 | tf_op jit(solution)/shard_map/ppermute | solution.py:365
  9.1 0.0 collective-permute-done.partner.refs_4_
  9.1 1.6 %collective-permute-start.3 = (f32[8,2432]{1,0:T(8,128)S(1)}, f32[8,2432]{1,0:T(8,128)S(1)}, u32[]{:S(2)}, u32[]{:S(2)}) collective-permute-start(f32[8,2432]{1,0:T(8,128)S(1)} %join.1.refs_0_), channel_id=1, source_target_pairs={{0,2},{1,3},{2,4},{3,5},{4,6},{5,7},{6,0},{7,1},{8,10},{9,11},{10,... | collective-permute-start | bytes 233480 | tf_op jit(solution)/shard_map/ppermute | solution.py:377
  10.7 2.6 %collective-permute-start.4 = (f32[8,2432]{1,0:T(8,128)S(1)}, f32[8,2432]{1,0:T(8,128)S(1)}, u32[]{:S(2)}, u32[]{:S(2)}) collective-permute-start(f32[8,2432]{1,0:T(8,128)S(1)} %join.1.refs_0_), channel_id=1, source_target_pairs={{0,4},{1,5},{2,6},{3,7},{4,0},{5,1},{6,2},{7,3},{8,12},{9,13},{10,... | collective-permute-start | bytes 233480 | tf_op jit(solution)/shard_map/ppermute | solution.py:377
  13.3 1.3 %collective-permute-start.5 = (f32[8,2432]{1,0:T(8,128)S(1)}, f32[8,2432]{1,0:T(8,128)S(1)}, u32[]{:S(2)}, u32[]{:S(2)}) collective-permute-start(f32[8,2432]{1,0:T(8,128)S(1)} %join.1.refs_0_), channel_id=1, source_target_pairs={{0,6},{1,7},{2,0},{3,1},{4,2},{5,3},{6,4},{7,5},{8,14},{9,15},{10,... | collective-permute-start | bytes 233480 | tf_op jit(solution)/shard_map/ppermute | solution.py:377
  16.0 0.0 copy-start
  16.0 0.2 collective-permute-done.3.refs_1_
  16.1 3.0 %collective-permute-done.4.refs_2_ = f32[8,2432]{1,0:T(8,128)S(1)} collective-permute-done((f32[8,2432]{1,0:T(8,128)S(1)}, f32[8,2432]{1,0:T(8,128)S(1)}, u32[]{:S(2)}, u32[]{:S(2)}) %collective-permute-start.4) | collective-permute-done | bytes 77856 | tf_op jit(solution)/shard_map/ppermute | solution.py:377
  19.2 0.1 collective-permute-done.5.refs_3_
  19.3 8.6 %pairs.1 = (f32[4,2048]{1,0:T(4,128)S(1)}, f32[4,2048]{1,0:T(4,128)S(1)}) custom-call(f32[8,2432]{1,0:T(8,128)S(1)} %join.1.refs_0_, f32[8,2432]{1,0:T(8,128)S(1)} %collective-permute-done.3.refs_1_, f32[8,2432]{1,0:T(8,128)S(1)} %collective-permute-done.4.refs_2_, f32[8,2432]{1,0:T(8,128)S(1)} %collective-permute-done.5.refs_3_, ...), custom_call_target="tpu_custom_call" | custom-call | tf_op jit(solution)/shard_map/pairs/pallas_call | solution.py:308
  27.9 0.1 collective-permute-start.6
  28.0 0.1 pad_maximum_fusion
  28.1 3.8 %collective-permute-done.6.other = f32[4,2048]{1,0:T(4,128)S(1)} collective-permute-done((f32[4,2048]{1,0:T(4,128)S(1)}, f32[4,2048]{1,0:T(4,128)S(1)}, u32[]{:S(2)}, u32[]{:S(2)}) %collective-permute-start.6) | collective-permute-done | bytes 32800 | tf_op jit(solution)/shard_map/ppermute | solution.py:381
  31.9 0.1 broadcast_in_dim.2.step
  31.9 0.0 copy-done
  31.9 0.7 %advance.1 = (f32[4,2048]{1,0:T(4,128)}, f32[7,2048]{1,0:T(8,128)}) custom-call(f32[2,128]{1,0:T(2,128)S(1)} %broadcast_in_dim.2.step, f32[8,2048]{1,0:T(8,128)S(1)} %copy-done, f32[4,2048]{1,0:T(4,128)S(1)} %get-tuple-element.8.own, f32[4,2048]{1,0:T(4,128)S(1)} %collective-permute-done.6.other), custom_call_target="tpu_custom_call" | custom-call | tf_op jit(solution)/shard_map/advance/pallas_call | solution.py:382
  (2 shorter events, 0.0 us)
Async XLA Ops:
  1.6 7.5 %collective-permute-start = (f32[8,2176]{1,0:T(8,128)S(1)}, f32[8,2176]{1,0:T(8,128)S(1)}, u32[]{:S(2)}, u32[]{:S(2)}) collective-permute-start(f32[8,2176]{1,0:T(8,128)S(1)} %pack.1.pair), channel_id=1, source_target_pairs={{0,1},{1,0},{2,3},{3,2},{4,5},{5,4},{6,7},{7,6},{8,9},{9,8},{10,11... | collective-permute-start | bytes 208904 | tf_op jit(solution)/shard_map/ppermute | solution.py:355
  5.9 1.7 %collective-permute-start.1 = (f32[8,128]{1,0:T(8,128)S(1)}, f32[8,128]{1,0:T(8,128)S(1)}, u32[]{:S(2)}, u32[]{:S(2)}) collective-permute-start(f32[8,128]{1,0:T(8,128)S(1)} %get-tuple-element.6), channel_id=1, source_target_pairs={{0,8},{8,0},{16,24},{24,16},{1,9},{9,1},{17,25},{25,17},{2,10},{10... | collective-permute-start | bytes 12296 | tf_op jit(solution)/shard_map/ppermute | solution.py:364
  6.0 3.1 %collective-permute-start.2 = (f32[8,128]{1,0:T(8,128)S(1)}, f32[8,128]{1,0:T(8,128)S(1)}, u32[]{:S(2)}, u32[]{:S(2)}) collective-permute-start(f32[8,128]{1,0:T(8,128)S(1)} %get-tuple-element.7), channel_id=1, source_target_pairs={{0,24},{8,16},{16,8},{24,0},{1,25},{9,17},{17,9},{25,1},{2,26},{10... | collective-permute-start | bytes 12296 | tf_op jit(solution)/shard_map/ppermute | solution.py:365
  9.1 7.1 %collective-permute-start.3 = (f32[8,2432]{1,0:T(8,128)S(1)}, f32[8,2432]{1,0:T(8,128)S(1)}, u32[]{:S(2)}, u32[]{:S(2)}) collective-permute-start(f32[8,2432]{1,0:T(8,128)S(1)} %join.1.refs_0_), channel_id=1, source_target_pairs={{0,2},{1,3},{2,4},{3,5},{4,6},{5,7},{6,0},{7,1},{8,10},{9,11},{10,... | collective-permute-start | bytes 233480 | tf_op jit(solution)/shard_map/ppermute | solution.py:377
  10.7 8.4 %collective-permute-start.4 = (f32[8,2432]{1,0:T(8,128)S(1)}, f32[8,2432]{1,0:T(8,128)S(1)}, u32[]{:S(2)}, u32[]{:S(2)}) collective-permute-start(f32[8,2432]{1,0:T(8,128)S(1)} %join.1.refs_0_), channel_id=1, source_target_pairs={{0,4},{1,5},{2,6},{3,7},{4,0},{5,1},{6,2},{7,3},{8,12},{9,13},{10,... | collective-permute-start | bytes 233480 | tf_op jit(solution)/shard_map/ppermute | solution.py:377
  13.3 6.0 %collective-permute-start.5 = (f32[8,2432]{1,0:T(8,128)S(1)}, f32[8,2432]{1,0:T(8,128)S(1)}, u32[]{:S(2)}, u32[]{:S(2)}) collective-permute-start(f32[8,2432]{1,0:T(8,128)S(1)} %join.1.refs_0_), channel_id=1, source_target_pairs={{0,6},{1,7},{2,0},{3,1},{4,2},{5,3},{6,4},{7,5},{8,14},{9,15},{10,... | collective-permute-start | bytes 233480 | tf_op jit(solution)/shard_map/ppermute | solution.py:377
  16.0 16.0 %copy-start = (f32[8,2048]{1,0:T(8,128)S(1)}, f32[8,2048]{1,0:T(8,128)}, u32[]{:S(2)}) copy-start(f32[8,2048]{1,0:T(8,128)} %particles.3) | copy-start | bytes 196612
  27.9 4.0 %collective-permute-start.6 = (f32[4,2048]{1,0:T(4,128)S(1)}, f32[4,2048]{1,0:T(4,128)S(1)}, u32[]{:S(2)}, u32[]{:S(2)}) collective-permute-start(f32[4,2048]{1,0:T(4,128)S(1)} %get-tuple-element.9), channel_id=1, source_target_pairs={{0,1},{1,0},{2,3},{3,2},{4,5},{5,4},{6,7},{7,6},{8,9},{9,8},{10,11... | collective-permute-start | bytes 98312 | tf_op jit(solution)/shard_map/ppermute | solution.py:381

commit v2 on v1

v2 whole, which is shorter than its diff:
```python
import functools

import jax
import jax.numpy as jnp
from jax import lax
from jax.experimental import pallas as pl
from jax.experimental.pallas import tpu as pltpu
from jax.sharding import PartitionSpec as P

PB = 128
BLK_DEV = 16

SMOOTHING = 1.0
KERNEL_NORM = 21.0 / (16.0 * 3.141592653589793)
SOUND_SPEED = 10.0
STIFFNESS = SOUND_SPEED * SOUND_SPEED / 7.0
VISCOSITY = 0.1
BLAST_STRENGTH = 8.0
DECAY_TIME = 8.0

KAPPA = (5.0 * KERNEL_NORM) ** (1.0 / 3.0)
SCALE = 0.5 * KAPPA
SCALE_SQ = SCALE * SCALE
CENTRE = 1.5
DENSITY_SCALE = -0.5 / (VISCOSITY * SOUND_SPEED * SMOOTHING * SCALE_SQ)
BATCH = 16
ROWS = 32

F32 = jnp.float32
BF16 = jnp.bfloat16
VMEM = pl.BlockSpec(memory_space=pltpu.VMEM)
SMEM = pl.BlockSpec(memory_space=pltpu.SMEM)
HBM = pl.BlockSpec(memory_space=pltpu.HBM)
PAIRS = pltpu.CompilerParams(vmem_limit_bytes=32 * 1024 * 1024)
SMALL = pltpu.CompilerParams(vmem_limit_bytes=4 * 1024 * 1024)


def split_3(value):
    first = value.astype(BF16).astype(F32)
    rest = value - first
    second = rest.astype(BF16).astype(F32)
    return first, second, rest - second


def stacked(parts, order):
    return [parts[k] for k in order]


def divided(value, by):
    if by & (by - 1) == 0:
        return lax.shift_right_logical(value, by.bit_length() - 1)
    return jnp.floor((value.astype(F32) + 0.5) * (1.0 / by)).astype(jnp.int32)


def pack_kernel(particles, first, second, live, pair_out, lists, sems):
    width = particles.shape[1]
    moves = [(values, lists.at[kind]) for kind, values in enumerate((first, second, live))]
    moves.append((particles, pair_out.at[:, 0:width]))
    copies = [pltpu.make_async_copy(*move, sems.at[k]) for k, move in enumerate(moves)]
    for copy in copies:
        copy.start()
    for copy in copies:
        copy.wait()
    pair_out[:, width : width + PB] = jnp.zeros((8, PB), F32)
    for kind in range(3):
        pair_out[kind : kind + 1, width : width + PB] = lists[kind].astype(F32)


def rim_kernel(up_ids, down_ids, pair, near_out, far_out):
    is_odd = lax.rem(lax.axis_index("slab"), 2)
    for item in range(up_ids.shape[0]):
        up, down = up_ids[item], down_ids[item]
        change = is_odd * (down - up)
        for number, out in ((up + change, near_out), (down - change, far_out)):
            start = pl.multiple_of(number * PB, PB)
            out[:, item * PB : (item + 1) * PB] = pair[:, pl.ds(start, PB)]


def join_kernel(pair, partner, near, far, column_out):
    width = pair.shape[1] - PB
    rim = near.shape[1]
    slab = lax.axis_index("slab")
    is_odd = lax.rem(slab, 2) == 1
    below = jnp.where(is_odd, near[...], far[...])
    above = jnp.where(is_odd, far[...], near[...])
    column_out[:, 0:width] = pair[:, 0:width]
    column_out[:, width : width + rim] = jnp.where(slab > 0, below, 0.0)
    column_out[:, width + rim : width + 2 * rim] = jnp.where(slab < lax.axis_size("slab") - 1, above, 0.0)
    column_out[:, width + 2 * rim :] = pair[:, width:]
    column_out[3:6, width + 2 * rim :] = partner[0:3, width:]


def pressure_term(density):
    term = STIFFNESS * (density**7 - 1.0) / (density * density)
    return jnp.where(density > 0.0, term, 0.0)


def add_tiles(codes, row, count, acting, summing, receiving, sums, products, parts):
    def work(first, lots):
        items = [codes[row, first + lot] for lot in range(lots)]
        targets = [lax.shift_right_logical(item, 10) for item in items]
        sources = [item & 1023 for item in items]
        for lot in range(lots):
            products[lot] = lax.dot_general(
                acting[sources[lot]],
                receiving[targets[lot]],
                (((0,), (0,)), ((), ())),
                preferred_element_type=F32,
            )
        closings = []
        for lot in range(lots):
            closing_sum = jnp.zeros((8, PB), F32)
            for start in range(0, PB, ROWS):
                span = slice(start, start + ROWS)
                dist_sq = jnp.maximum(products[lot, span, 0:PB], 1e-12)
                approach = products[lot, span, PB : 2 * PB]
                support = jnp.maximum(KAPPA - dist_sq * lax.rsqrt(dist_sq), 0.0)
                gradient = support * support * support
                closing = approach * gradient
                weight = (dist_sq + 0.01 * SMOOTHING * SMOOTHING * SCALE_SQ) * products[
                    lot, span, 2 * PB : 3 * PB
                ]
                damping = jnp.minimum(approach, 0.0) * pl.reciprocal(weight, approx=True)
                push = (products[lot, span, 3 * PB :] + damping) * gradient
                high = push.astype(BF16)
                parts[lot, start : start + ROWS, :] = high
                parts[lot, PB + start : PB + start + ROWS, :] = (push - high.astype(F32)).astype(BF16)
                for part in range(0, ROWS, 8):
                    closing_sum = closing_sum + closing[part : part + 8]
            closings.append(closing_sum)
        for lot in range(lots):
            total = jnp.dot(summing[sources[lot]], parts[lot], preferred_element_type=F32)
            sums[targets[lot], 0:8, :] += closings[lot]
            sums[targets[lot], 8:16, :] += total[0:8] + total[8:16] + total[16:24]

    def full(turn, carry):
        work(turn * BATCH, BATCH)
        return carry

    half = BATCH // 2
    turns = lax.div(count + half - 1, BATCH)
    lax.fori_loop(0, turns, full, 0)

    @pl.when(count > turns * BATCH)
    def _():
        work(turns * BATCH, half)


def write_rates(sums, base, source, out):
    for block in range(BLK_DEV):
        number, place = base + block, slice(block * PB, (block + 1) * PB)
        out[0:1, place] = -jnp.sum(sums[number, 0:8, :], axis=0, keepdims=True)
        out[1:4, place] = (source[0:3, place] - CENTRE) * sums[number, 11:12, :] - sums[number, 8:11, :]


FIRST_ORDER, SECOND_ORDER = (0, 1, 0, 1, 2, 0), (0, 0, 1, 1, 0, 2)


def row_8():
    return lax.broadcasted_iota(jnp.int32, (8, PB), 0)


def fields(block):
    moved = block - jnp.where(row_8() < 3, CENTRE, 0.0)
    scaled = moved * jnp.where(row_8() < 3, SCALE, 0.0)
    norm = jnp.sum(scaled * scaled, axis=0, keepdims=True)
    inner = jnp.sum(moved[0:3] * moved[3:6], axis=0, keepdims=True)
    density = block[6:7]
    return moved, scaled, norm, inner, density * DENSITY_SCALE, pressure_term(density), block[7:8]


def by_row(*rows):
    value = rows[-1]
    for row, other in zip(range(len(rows) - 2, -1, -1), rows[-2::-1]):
        value = jnp.where(row_8() == row, other, value)
    return value


def columns_of(near, meet, rest, orders):
    rows = stacked(split_3(near), orders) + stacked(split_3(meet), orders)
    rows += stacked(split_3(rest), orders[:3]) + [jnp.zeros((8, PB), F32)]
    return jnp.concatenate(rows, axis=0).astype(BF16)


def prepare_receiving(receiving, number, block):
    moved, scaled, norm, inner, density, pressure, mass = fields(block)
    near = jnp.where(row_8() < 3, scaled, by_row(0.0, 0.0, 0.0, norm, 1.0, 0.0))
    blank = jnp.zeros((8, PB), F32)
    meet = jnp.concatenate([moved[3:6], moved[0:3], inner, jnp.ones((1, PB), F32)], axis=0)
    sparse = [
        columns_of(near, blank, blank, SECOND_ORDER),
        columns_of(blank, meet, blank, SECOND_ORDER),
        columns_of(blank, blank, by_row(density, 1.0, 0.0), SECOND_ORDER),
        columns_of(blank, blank, by_row(0.0, 0.0, pressure, 1.0, 0.0), SECOND_ORDER),
    ]
    for k in range(4):
        receiving[number, :, k * PB : (k + 1) * PB] = sparse[k]


def prepare_acting(acting, summing, number, block):
    blank = jnp.zeros((8, PB), F32)
    moved, scaled, norm, inner, density, pressure, mass = fields(block)
    near = jnp.where(row_8() < 3, -2.0 * scaled, by_row(0.0, 0.0, 0.0, 1.0, norm, 0.0))
    meet = jnp.where(row_8() < 6, -moved, jnp.where(row_8() == 6, 1.0, inner)) * mass
    rest = by_row(1.0, density, mass, mass * pressure, 0.0)
    acting[number] = columns_of(near, meet, rest, FIRST_ORDER)
    spot = split_3(jnp.where(row_8() < 3, moved, jnp.where(row_8() == 3, 1.0, 0.0)))
    summing[number, :, 0:PB] = jnp.concatenate([*spot, blank], axis=0).astype(BF16)
    summing[number, :, PB:] = jnp.concatenate([spot[0], spot[1], blank, blank], axis=0).astype(BF16)


def find_tiles(columns, early, rim, lists, codes, is_early, sides):
    shifts = lax.axis_size("tile") // 2
    dev_blocks = BLK_DEV + 2 * rim
    tile = lax.axis_index("tile")
    row, column = lax.div(tile, 2), lax.rem(tile, 2)
    list_start = dev_blocks * PB
    places = list(columns)
    holders = 2 * len(places)
    for position, shift in enumerate(places):
        for side in range(2):
            for kind in range(3):
                lists[kind, 2 * position + side : 2 * position + side + 1, :] = columns[shift][
                    3 * side + kind : 3 * side + kind + 1, list_start : list_start + PB
                ]
    first = lists[0, 0:holders].astype(jnp.int32)
    second = lists[1, 0:holders].astype(jnp.int32)
    slab_blocks = 2 * shifts * BLK_DEV
    is_rim = second >= slab_blocks
    rim_number = second - slab_blocks
    is_above = rim_number >= 2 * shifts * rim
    rim_number = jnp.where(is_above, rim_number - 2 * shifts * rim, rim_number)
    rim_owner = divided(rim_number, rim)
    owner = jnp.where(is_rim, rim_owner, divided(second, BLK_DEV))
    place = jnp.where(
        is_rim,
        BLK_DEV + rim_number - rim_owner * rim + jnp.where(is_above, rim, 0),
        second & (BLK_DEV - 1),
    )
    behind = row - divided(owner, 2)
    behind = jnp.where(behind < 0, behind + shifts, behind)
    arrival = jnp.zeros_like(behind)
    for position, shift in enumerate(places):
        arrival = jnp.where(behind == shift, position, arrival)
    target = divided(first, BLK_DEV)
    mine = (lists[2, 0:holders] > 0.5) & (divided(target, 2) == row) & ((owner & 1) == column)
    from_early = functools.reduce(jnp.logical_or, [behind == shift for shift in early])
    if is_early:
        mine = mine & from_early
    else:
        held_early = lax.broadcasted_iota(jnp.int32, (holders, PB), 0) < 2 * len(early)
        mine = mine & jnp.logical_not(from_early & held_early)
    is_own = (target & 1) == column
    code = ((first & (BLK_DEV - 1)) + jnp.where(is_own, BLK_DEV, 0)) * 1024 + arrival * dev_blocks + place + 1
    chosen = mine if sides == 1 else jnp.concatenate([mine & jnp.logical_not(is_own), mine & is_own], axis=0)
    lane = lax.broadcasted_iota(jnp.int32, (PB, PB), 1)
    sublane = lax.broadcasted_iota(jnp.int32, (PB, PB), 0)
    ones = jnp.where(chosen, 1.0, 0.0)
    before = jnp.where(sublane < lane, 1.0, 0.0).astype(BF16)
    rank = jnp.dot(ones.astype(BF16), before, preferred_element_type=F32)
    counts = jnp.sum(ones, axis=1, keepdims=True)
    slots = codes.shape[1]
    spots = lax.broadcasted_iota(jnp.int32, (slots, PB), 0)
    for side in range(sides):
        found = jnp.zeros((slots, PB), jnp.int32)
        offset = jnp.zeros((1, 1), F32)
        for holder in range(holders):
            line = slice(side * holders + holder, side * holders + holder + 1)
            order = jnp.where(chosen[line], (rank[line] + offset).astype(jnp.int32), -1)
            found = jnp.where(spots == order, code[holder : holder + 1], found)
            offset = offset + counts[line]
        codes[2 + side : 3 + side, :] = jnp.broadcast_to(offset, (1, slots)).astype(jnp.int32)
        row_sum = jnp.ones((8, PB), BF16)
        high, low = (
            lax.dot_general(
                row_sum, part.astype(F32).astype(BF16), (((1,), (1,)), ((), ())), preferred_element_type=F32
            )
            for part in (lax.shift_right_logical(found, 8), found & 255)
        )
        total = high[0:1].astype(jnp.int32) * 256 + low[0:1].astype(jnp.int32)
        codes[side : side + 1, :] = jnp.where(total == 0, 2 * BLK_DEV * 1024, total - 1)


def block_at(ref, number):
    return ref[:, pl.ds(pl.multiple_of(number * PB, PB), PB)]


def prepare_all_acting(acting, summing, columns, dev_blocks):
    def each(number, carry):
        for position, column in enumerate(columns):
            prepare_acting(acting, summing, position * dev_blocks + number, block_at(column, number))
        return carry

    lax.fori_loop(0, dev_blocks, each, 0)


def early_kernel(early, rim, *refs):
    columns = refs[: len(early)]
    partner, receiving, sums, acting, summing, products, parts, lists, codes, codes_smem, sem = refs[len(early) :]
    find_tiles(dict(zip(early, columns)), early, rim, lists, codes, True, 1)
    copy = pltpu.make_async_copy(codes, codes_smem, sem)
    copy.start()

    def each_receiving(number, carry):
        prepare_receiving(receiving, number, block_at(partner, number))
        prepare_receiving(receiving, BLK_DEV + number, block_at(columns[0], number))
        return carry

    lax.fori_loop(0, BLK_DEV, each_receiving, 0)
    receiving[2 * BLK_DEV] = jnp.zeros(receiving.shape[1:], BF16)
    prepare_all_acting(acting, summing, columns, BLK_DEV + 2 * rim)
    sums[...] = jnp.zeros(sums.shape, F32)
    copy.wait()
    add_tiles(codes_smem, 0, codes_smem[2, 0], acting, summing, receiving, sums, products, parts)


def other_kernel(arrivals, early, rim, *refs):
    columns = refs[: len(arrivals)]
    partner, receiving, sums_in, other_out, codes, acting, summing = refs[len(arrivals) : len(arrivals) + 7]
    sums, products, parts, lists, codes_smem, sem = refs[len(arrivals) + 7 :]
    find_tiles(dict(zip(arrivals, columns)), early, rim, lists, codes, False, 2)
    copy = pltpu.make_async_copy(codes, codes_smem, sem)
    copy.start()
    prepare_all_acting(acting, summing, columns, BLK_DEV + 2 * rim)
    sums[...] = sums_in[...]
    copy.wait()
    add_tiles(codes_smem, 0, codes_smem[2, 0], acting, summing, receiving, sums, products, parts)
    write_rates(sums, 0, partner, other_out)


def own_kernel(
    codes, acting, summing, receiving, sums_in, column, own_out, sums, products, parts, codes_smem, sem
):
    copy = pltpu.make_async_copy(codes, codes_smem, sem)
    copy.start()
    sums[...] = sums_in[...]
    copy.wait()
    add_tiles(codes_smem, 1, codes_smem[3, 0], acting, summing, receiving, sums, products, parts)
    write_rates(sums, BLK_DEV, column, own_out)


def advance_kernel(step, particles, own, other, rates_out, advanced_out):
    step_length = step[0:1]
    elapsed = step[1:2] * step_length
    strength = BLAST_STRENGTH * jnp.exp(-elapsed / DECAY_TIME)
    step_length, strength = step_length[:, 0:1], strength[:, 0:1]
    block = particles[...]
    tile_rates = own[...] + other[...]
    relative = block[0:3] + 1.0
    spread_sq = jnp.sum(relative * relative, axis=0, keepdims=True) + 1.0
    source = strength * relative / (spread_sq * jnp.sqrt(spread_sq))
    forcing = tile_rates[1:4] + source
    rates_out[0:1] = tile_rates[0:1]
    rates_out[1:4] = forcing
    velocity = block[3:6] + step_length * forcing
    advanced_out[0:3] = block[0:3] + step_length * velocity
    advanced_out[3:6] = velocity
    advanced_out[6:7] = block[6:7] + step_length * tile_rates[0:1]


def pair_sums(arrivals, columns, partner, rim):
    width = partner.shape[1] - PB
    dev_blocks = BLK_DEV + 2 * rim
    early = arrivals[:2]
    partial = jax.ShapeDtypeStruct((4, width), F32)
    receiving = jax.ShapeDtypeStruct((2 * BLK_DEV + 1, PB, 4 * PB), BF16)
    sums = jax.ShapeDtypeStruct((2 * BLK_DEV + 1, 16, PB), F32)
    batch_scratch = [pltpu.VMEM((BATCH, PB, 4 * PB), F32), pltpu.VMEM((BATCH, 2 * PB, PB), BF16)]

    def actors(shifts):
        count = len(shifts) * dev_blocks
        return (count, PB, PB), (count, 32, 2 * PB)

    def tables(shifts, slots):
        code = (8, slots)
        return pltpu.VMEM((3, 2 * len(shifts), PB), F32), pltpu.SMEM(code, jnp.int32), pltpu.SemaphoreType.DMA

    lists, codes_smem, sem = tables(early, 2 * PB)
    receiving, sums = pl.pallas_call(
        functools.partial(early_kernel, early, rim),
        out_shape=(receiving, sums),
        in_specs=[VMEM] * (len(early) + 1),
        out_specs=[VMEM] * 2,
        scratch_shapes=[
            *(pltpu.VMEM(shape, BF16) for shape in actors(early)),
            *batch_scratch,
            lists,
            pltpu.VMEM((8, 2 * PB), jnp.int32),
            codes_smem,
            sem,
        ],
        compiler_params=PAIRS,
        cost_estimate=pl.CostEstimate(flops=8_000_000, bytes_accessed=8_000_000, transcendentals=0),
        name="pairs_early",
    )(*(columns[shift] for shift in early), partner)
    lists, codes_smem, sem = tables(arrivals, PB)
    other, *prepared = pl.pallas_call(
        functools.partial(other_kernel, arrivals, early, rim),
        out_shape=(
            partial,
            jax.ShapeDtypeStruct((8, PB), jnp.int32),
            *(jax.ShapeDtypeStruct(shape, BF16) for shape in actors(arrivals)),
        ),
        in_specs=[VMEM] * (len(arrivals) + 3),
        out_specs=[VMEM] * 4,
        scratch_shapes=[pltpu.VMEM(sums.shape, F32), *batch_scratch, lists, codes_smem, sem],
        compiler_params=PAIRS,
        name="pairs_other",
    )(*(columns[shift] for shift in arrivals), partner, receiving, sums)

    def own():
        return pl.pallas_call(
            own_kernel,
            out_shape=partial,
            in_specs=[VMEM] * 6,
            out_specs=VMEM,
            scratch_shapes=[pltpu.VMEM(sums.shape, F32), *batch_scratch, codes_smem, sem],
            compiler_params=PAIRS,
            name="pairs_own",
        )(*prepared, receiving, sums, columns[0])

    return other, own


def on_device(
    particles, halo_up, halo_down, tile_first, tile_second, tile_live, step_index, time_step
):
    width = particles.shape[1]
    rim = halo_up.shape[0]
    rim_width = rim * PB
    tiles, slabs = lax.axis_size("tile"), lax.axis_size("slab")
    shifts = tiles // 2
    given = (particles, tile_first, tile_second, tile_live)
    given = [pltpu.with_memory_space_constraint(array, pltpu.HBM) for array in given]
    pair = pl.pallas_call(
        pack_kernel,
        out_shape=jax.ShapeDtypeStruct((8, width + PB), F32),
        in_specs=[HBM] * 4,
        out_specs=VMEM,
        scratch_shapes=[
            pltpu.VMEM((3, 1, tile_first.shape[-1]), jnp.int32),
            pltpu.SemaphoreType.DMA((4,)),
        ],
        compiler_params=SMALL,
        name="pack",
    )(*given)
    across = [(i, i ^ 1) for i in range(tiles)]
    evens = [(i, i ^ 1) for i in range(slabs)]
    odds = [(i, (i + 1 if i % 2 else i - 1) % slabs) for i in range(slabs)]
    partner = lax.ppermute(pair, "tile", across)
    near, far = pl.pallas_call(
        rim_kernel,
        out_shape=[jax.ShapeDtypeStruct((8, rim_width), F32)] * 2,
        in_specs=[SMEM, SMEM, VMEM],
        out_specs=(VMEM, VMEM),
        compiler_params=SMALL,
        name="rim",
    )(halo_up, halo_down, pair)
    near = lax.ppermute(near, "slab", evens)
    far = lax.ppermute(far, "slab", odds)
    column = pl.pallas_call(
        join_kernel,
        out_shape=jax.ShapeDtypeStruct((8, width + 2 * rim_width + PB), F32),
        in_specs=[VMEM] * 4,
        out_specs=VMEM,
        compiler_params=SMALL,
        name="join",
    )(pair, partner, near, far)
    columns = [column] * shifts
    arrivals = tuple(range(shifts))
    for shift in arrivals[1:]:
        ring = [(i, (i + 2 * shift) % tiles) for i in range(tiles)]
        columns[shift] = lax.ppermute(column, "tile", ring)
    other, own = pair_sums(arrivals, columns, partner, rim)
    step = jnp.concatenate([time_step, step_index.astype(F32)])
    step = jnp.broadcast_to(step[:, None], (2, PB))
    other = lax.ppermute(other, "tile", across)
    return pl.pallas_call(
        advance_kernel,
        out_shape=(
            jax.ShapeDtypeStruct((4, width), F32),
            jax.ShapeDtypeStruct((7, width), F32),
        ),
        in_specs=[VMEM] * 4,
        out_specs=(VMEM, VMEM),
        compiler_params=SMALL,
        name="advance",
    )(step, particles, own(), other)


def solution(mesh):
    placed = (
        P(None, ("slab", "tile")),
        P(("slab", "tile")),
        P(("slab", "tile")),
        P("slab", "tile"),
        P("slab", "tile"),
        P("slab", "tile"),
        P(),
        P(),
    )
    return jax.shard_map(
        on_device,
        mesh=mesh,
        in_specs=placed,
        out_specs=(P(None, ("slab", "tile")), P(None, ("slab", "tile"))),
        check_vma=False,
    )
```

time: 32.6 us -> 28.6 us (0.88)
  waiting for transfers between devices: 8.59 us -> 3.67 us
  Pallas kernels: 10.3 us -> 11.2 us
    ppermute x3, waiting for transfers between devices: 3.31 us -> 0.19 us  [on_device(): columns[shift] = lax.ppermute(column, 'tile', ring)]
    ppermute x1, waiting for transfers between devices: 3.82 us -> 2.01 us  [on_device(): other = lax.ppermute(other, 'tile', across)]
    pallas_call x1 -> x3, Pallas kernels: 8.61 us -> 9.51 us  [the longest x1 4.37 us: pair_sums(): pl.pallas_call(functools.partial(other_kernel, arrivals, early, rim), out...]
  transfers between devices with their start and end apart: 7 -> 7, of which waited for: 5 -> 3; matrix products, arithmetic and copies ran while one was open for 0% -> 0% of each run, Pallas kernels for 0% -> 18%
where the time goes in v2:
time: 28.6 us; the launch traced here: 28.7 us
  Pallas kernels  11.2 us (39%)
  starting transfers between devices  10.3 us (36%)
  waiting for transfers between devices  3.67 us (13%)
  between operations  3.31 us (12%)
    ppermute x3, starting transfers between devices, on_device(): columns[shift] = lax.ppermute(column, 'tile', ring)  5.57 us
    pallas_call x1, Pallas kernels, pair_sums(): pl.pallas_call(functools.partial(other_kernel, arrivals, early, rim), out...  4.37 us
    pallas_call x1, Pallas kernels, pair_sums(): pl.pallas_call(functools.partial(early_kernel, early, rim), out_shape=(re...  3.33 us
    ppermute x1, starting transfers between devices, on_device(): partner = lax.ppermute(pair, 'tile', across)  3 us
    ppermute x1, waiting for transfers between devices, on_device(): other = lax.ppermute(other, 'tile', across)  2.01 us
    pallas_call x1, Pallas kernels, own(): pl.pallas_call(own_kernel, out_shape=partial, in_specs=[VMEM] * 6, out_sp...  1.8 us
    ppermute x1, starting transfers between devices, on_device(): far = lax.ppermute(far, 'slab', odds)  1.64 us
    ppermute x1, waiting for transfers between devices, on_device(): far = lax.ppermute(far, 'slab', odds)  1.46 us
  transfers between devices with their start and end apart: 7, of which 3 were waited for; matrix products, arithmetic and copies ran while one was open for 0% of the time, Pallas kernels for 18%

profile of v2, /device:TPU:0, one launch (start us, length us, event | category | flops | bytes accessed | tf_op | source)
XLA Modules:
  0.0 28.7 jit_solution(7572645788741169042)
XLA Ops:
  0.6 0.9 %pack.1.pair = f32[8,2176]{1,0:T(8,128)S(1)} custom-call(f32[8,2048]{1,0:T(8,128)} %particles.3, s32[1,128]{1,0:T(1,128)} %first.1, s32[1,128]{1,0:T(1,128)} %second.1, s32[1,128]{1,0:T(1,128)} %live.1), custom_call_target="tpu_custom_call" | custom-call | tf_op jit(solution)/shard_map/pack/pallas_call | solution.py:435
  1.6 3.0 %collective-permute-start = (f32[8,2176]{1,0:T(8,128)S(1)}, f32[8,2176]{1,0:T(8,128)S(1)}, u32[]{:S(2)}, u32[]{:S(2)}) collective-permute-start(f32[8,2176]{1,0:T(8,128)S(1)} %pack.1.pair), channel_id=1, source_target_pairs={{0,1},{1,0},{2,3},{3,2},{4,5},{5,4},{6,7},{7,6},{8,9},{9,8},{10,11... | collective-permute-start | bytes 208904 | tf_op jit(solution)/shard_map/ppermute | solution.py:450
  5.9 0.1 collective-permute-start.1
  6.0 1.6 %collective-permute-start.2 = (f32[8,128]{1,0:T(8,128)S(1)}, f32[8,128]{1,0:T(8,128)S(1)}, u32[]{:S(2)}, u32[]{:S(2)}) collective-permute-start(f32[8,128]{1,0:T(8,128)S(1)} %get-tuple-element.11), channel_id=1, source_target_pairs={{0,24},{8,16},{16,8},{24,0},{1,25},{9,17},{17,9},{25,1},{2,26},{10... | collective-permute-start | bytes 12296 | tf_op jit(solution)/shard_map/ppermute | solution.py:460
  7.6 0.0 collective-permute-done.1.near
  7.6 1.5 %collective-permute-done.2.far = f32[8,128]{1,0:T(8,128)S(1)} collective-permute-done((f32[8,128]{1,0:T(8,128)S(1)}, f32[8,128]{1,0:T(8,128)S(1)}, u32[]{:S(2)}, u32[]{:S(2)}) %collective-permute-start.2) | collective-permute-done | bytes 4128 | tf_op jit(solution)/shard_map/ppermute | solution.py:460
  9.1 0.0 collective-permute-done.partner.refs_2_.refs_4_
  9.1 1.6 %collective-permute-start.3 = (f32[8,2432]{1,0:T(8,128)S(1)}, f32[8,2432]{1,0:T(8,128)S(1)}, u32[]{:S(2)}, u32[]{:S(2)}) collective-permute-start(f32[8,2432]{1,0:T(8,128)S(1)} %join.1.refs_0_.column), channel_id=1, source_target_pairs={{0,2},{1,3},{2,4},{3,5},{4,6},{5,7},{6,0},{7,1},{8,10},{9,11},{10,... | collective-permute-start | bytes 233480 | tf_op jit(solution)/shard_map/ppermute | solution.py:473
  10.7 2.6 %collective-permute-start.4 = (f32[8,2432]{1,0:T(8,128)S(1)}, f32[8,2432]{1,0:T(8,128)S(1)}, u32[]{:S(2)}, u32[]{:S(2)}) collective-permute-start(f32[8,2432]{1,0:T(8,128)S(1)} %join.1.refs_0_.column), channel_id=1, source_target_pairs={{0,4},{1,5},{2,6},{3,7},{4,0},{5,1},{6,2},{7,3},{8,12},{9,13},{10,... | collective-permute-start | bytes 233480 | tf_op jit(solution)/shard_map/ppermute | solution.py:473
  13.3 1.3 %collective-permute-start.5 = (f32[8,2432]{1,0:T(8,128)S(1)}, f32[8,2432]{1,0:T(8,128)S(1)}, u32[]{:S(2)}, u32[]{:S(2)}) collective-permute-start(f32[8,2432]{1,0:T(8,128)S(1)} %join.1.refs_0_.column), channel_id=1, source_target_pairs={{0,6},{1,7},{2,0},{3,1},{4,2},{5,3},{6,4},{7,5},{8,14},{9,15},{10,... | collective-permute-start | bytes 233480 | tf_op jit(solution)/shard_map/ppermute | solution.py:473
  16.0 0.2 collective-permute-done.3.refs_1_
  16.1 3.3 %pairs_early.1 = (bf16[33,128,512]{2,1,0:T(8,128)(2,1)S(1)}, f32[33,16,128]{2,1,0:T(8,128)S(1)}) custom-call(f32[8,2432]{1,0:T(8,128)S(1)} %join.1.refs_0_.column, f32[8,2432]{1,0:T(8,128)S(1)} %collective-permute-done.3.refs_1_, f32[8,2176]{1,0:T(8,128)S(1)} %collective-permute-done.partner.refs_2_.refs_4_), custom_call_target="tpu_custom_call" | custom-call | flops 8000000 | bytes 8000000 | tf_op jit(solution)/shard_map/pairs_early/pallas_call | solution.py:379
  19.5 0.0 collective-permute-done.4.refs_2_
  19.5 0.0 collective-permute-done.5.refs_3_
  19.5 4.4 %pairs_other.1 = (f32[4,2048]{1,0:T(4,128)S(1)}, s32[8,128]{1,0:T(8,128)S(1)}, bf16[72,128,128]{2,1,0:T(8,128)(2,1)S(1)}, bf16[72,32,256]{2,1,0:T(8,128)(2,1)S(1)}) custom-call(f32[8,2432]{1,0:T(8,128)S(1)} %join.1.refs_0_.column, f32[8,2432]{1,0:T(8,128)S(1)} %collective-permute-done.3.refs_1_, f32[8,2432]{1,0:T(8,128)S(1)} %collective-permute-done.4.refs_2_, ...), custom_call_target="tpu_custom_call" | custom-call | tf_op jit(solution)/shard_map/pairs_other/pallas_call | solution.py:397
  23.9 0.1 collective-permute-start.6
  24.0 0.1 pad_maximum_fusion
  24.1 0.0 copy-start
  24.1 1.8 %pairs_own.1.own = f32[4,2048]{1,0:T(4,128)S(1)} custom-call(s32[8,128]{1,0:T(8,128)S(1)} %get-tuple-element.14.codes, bf16[72,128,128]{2,1,0:T(8,128)(2,1)S(1)} %get-tuple-element.15.acting, bf16[72,32,256]{2,1,0:T(8,128)(2,1)S(1)} %get-tuple-element.16.summing, bf16[33,128,512]{2,1,0:T(8,128)(2,1)S(1)} %get-tuple-element.12.refs_5_.receiving, ...), custom_call_target="tpu_custom_call" | custom-call | tf_op jit(solution)/shard_map/pairs_own/pallas_call | solution.py:412
  25.9 2.0 %collective-permute-done.6.other = f32[4,2048]{1,0:T(4,128)S(1)} collective-permute-done((f32[4,2048]{1,0:T(4,128)S(1)}, f32[4,2048]{1,0:T(4,128)S(1)}, u32[]{:S(2)}, u32[]{:S(2)}) %collective-permute-start.6) | collective-permute-done | bytes 32800 | tf_op jit(solution)/shard_map/ppermute | solution.py:477
  27.9 0.1 broadcast_in_dim.2.step
  27.9 0.0 copy-done
  27.9 0.7 %advance.1 = (f32[4,2048]{1,0:T(4,128)}, f32[7,2048]{1,0:T(8,128)}) custom-call(f32[2,128]{1,0:T(2,128)S(1)} %broadcast_in_dim.2.step, f32[8,2048]{1,0:T(8,128)S(1)} %copy-done, f32[4,2048]{1,0:T(4,128)S(1)} %pairs_own.1.own, f32[4,2048]{1,0:T(4,128)S(1)} %collective-permute-done.6.other), custom_call_target="tpu_custom_call" | custom-call | tf_op jit(solution)/shard_map/advance/pallas_call | solution.py:478
  (2 shorter events, 0.0 us)
Async XLA Ops:
  1.6 7.5 %collective-permute-start = (f32[8,2176]{1,0:T(8,128)S(1)}, f32[8,2176]{1,0:T(8,128)S(1)}, u32[]{:S(2)}, u32[]{:S(2)}) collective-permute-start(f32[8,2176]{1,0:T(8,128)S(1)} %pack.1.pair), channel_id=1, source_target_pairs={{0,1},{1,0},{2,3},{3,2},{4,5},{5,4},{6,7},{7,6},{8,9},{9,8},{10,11... | collective-permute-start | bytes 208904 | tf_op jit(solution)/shard_map/ppermute | solution.py:450
  5.9 1.7 %collective-permute-start.1 = (f32[8,128]{1,0:T(8,128)S(1)}, f32[8,128]{1,0:T(8,128)S(1)}, u32[]{:S(2)}, u32[]{:S(2)}) collective-permute-start(f32[8,128]{1,0:T(8,128)S(1)} %get-tuple-element.10), channel_id=1, source_target_pairs={{0,8},{8,0},{16,24},{24,16},{1,9},{9,1},{17,25},{25,17},{2,10},{10... | collective-permute-start | bytes 12296 | tf_op jit(solution)/shard_map/ppermute | solution.py:459
  6.0 3.1 %collective-permute-start.2 = (f32[8,128]{1,0:T(8,128)S(1)}, f32[8,128]{1,0:T(8,128)S(1)}, u32[]{:S(2)}, u32[]{:S(2)}) collective-permute-start(f32[8,128]{1,0:T(8,128)S(1)} %get-tuple-element.11), channel_id=1, source_target_pairs={{0,24},{8,16},{16,8},{24,0},{1,25},{9,17},{17,9},{25,1},{2,26},{10... | collective-permute-start | bytes 12296 | tf_op jit(solution)/shard_map/ppermute | solution.py:460
  9.1 7.1 %collective-permute-start.3 = (f32[8,2432]{1,0:T(8,128)S(1)}, f32[8,2432]{1,0:T(8,128)S(1)}, u32[]{:S(2)}, u32[]{:S(2)}) collective-permute-start(f32[8,2432]{1,0:T(8,128)S(1)} %join.1.refs_0_.column), channel_id=1, source_target_pairs={{0,2},{1,3},{2,4},{3,5},{4,6},{5,7},{6,0},{7,1},{8,10},{9,11},{10,... | collective-permute-start | bytes 233480 | tf_op jit(solution)/shard_map/ppermute | solution.py:473
  10.7 8.8 %collective-permute-start.4 = (f32[8,2432]{1,0:T(8,128)S(1)}, f32[8,2432]{1,0:T(8,128)S(1)}, u32[]{:S(2)}, u32[]{:S(2)}) collective-permute-start(f32[8,2432]{1,0:T(8,128)S(1)} %join.1.refs_0_.column), channel_id=1, source_target_pairs={{0,4},{1,5},{2,6},{3,7},{4,0},{5,1},{6,2},{7,3},{8,12},{9,13},{10,... | collective-permute-start | bytes 233480 | tf_op jit(solution)/shard_map/ppermute | solution.py:473
  13.3 6.2 %collective-permute-start.5 = (f32[8,2432]{1,0:T(8,128)S(1)}, f32[8,2432]{1,0:T(8,128)S(1)}, u32[]{:S(2)}, u32[]{:S(2)}) collective-permute-start(f32[8,2432]{1,0:T(8,128)S(1)} %join.1.refs_0_.column), channel_id=1, source_target_pairs={{0,6},{1,7},{2,0},{3,1},{4,2},{5,3},{6,4},{7,5},{8,14},{9,15},{10,... | collective-permute-start | bytes 233480 | tf_op jit(solution)/shard_map/ppermute | solution.py:473
  23.9 4.0 %collective-permute-start.6 = (f32[4,2048]{1,0:T(4,128)S(1)}, f32[4,2048]{1,0:T(4,128)S(1)}, u32[]{:S(2)}, u32[]{:S(2)}) collective-permute-start(f32[4,2048]{1,0:T(4,128)S(1)} %get-tuple-element.17), channel_id=1, source_target_pairs={{0,1},{1,0},{2,3},{3,2},{4,5},{5,4},{6,7},{7,6},{8,9},{9,8},{10,11... | collective-permute-start | bytes 98312 | tf_op jit(solution)/shard_map/ppermute | solution.py:477
  24.1 3.9 %copy-start = (f32[8,2048]{1,0:T(8,128)S(1)}, f32[8,2048]{1,0:T(8,128)}, u32[]{:S(2)}) copy-start(f32[8,2048]{1,0:T(8,128)} %particles.3) | copy-start | bytes 196612

commit v3 on v2

--- a/solution.py
+++ b/solution.py
@@ -76,7 +76,7 @@
             out[:, item * PB : (item + 1) * PB] = pair[:, pl.ds(start, PB)]
 
 
-def join_kernel(pair, partner, near, far, column_out):
+def join_kernel(pair, partner, far, near, column_out):
     width = pair.shape[1] - PB
     rim = near.shape[1]
     slab = lax.axis_index("slab")
@@ -456,8 +456,8 @@
         compiler_params=SMALL,
         name="rim",
     )(halo_up, halo_down, pair)
+    far = lax.ppermute(far, "slab", odds)
     near = lax.ppermute(near, "slab", evens)
-    far = lax.ppermute(far, "slab", odds)
     column = pl.pallas_call(
         join_kernel,
         out_shape=jax.ShapeDtypeStruct((8, width + 2 * rim_width + PB), F32),
@@ -465,7 +465,7 @@
         out_specs=VMEM,
         compiler_params=SMALL,
         name="join",
-    )(pair, partner, near, far)
+    )(pair, partner, far, near)
     columns = [column] * shifts
     arrivals = tuple(range(shifts))
     for shift in arrivals[1:]:

time: 28.6 us -> 27.9 us (0.976); the launches traced: 28.7 us -> 27.7 us
  waiting for transfers between devices: 3.67 us -> 2.9 us
  Pallas kernels: 11.2 us -> 10.5 us
  starting transfers between devices: 10.3 us -> 10.9 us
    pallas_call x1, Pallas kernels: 4.37 us -> 3.23 us  [pair_sums(): pl.pallas_call(functools.partial(other_kernel, arrivals, early, rim), out...]
    ppermute x1, starting transfers between devices: 1.64 us -> 0.74 us  [on_device(): far = lax.ppermute(far, 'slab', odds)]
    ppermute x1, starting transfers between devices: 0.07 us -> 0.96 us  [on_device(): near = lax.ppermute(near, 'slab', evens)]
    ppermute x1, starting transfers between devices: 0.07 us -> 0.6 us  [on_device(): other = lax.ppermute(other, 'tile', across)]
    ppermute x1, waiting for transfers between devices: 2.01 us -> 1.49 us  [on_device(): other = lax.ppermute(other, 'tile', across)]
    pallas_call x1, Pallas kernels: 3.33 us -> 3.73 us  [pair_sums(): pl.pallas_call(functools.partial(early_kernel, early, rim), out_shape=(re...]
  transfers between devices with their start and end apart: 7 -> 7, of which waited for: 3 -> 2; matrix products, arithmetic and copies ran while one was open for 0% -> 0% of each run, Pallas kernels for 18% -> 20%
where the time goes in v3:
time: 27.9 us; the launch traced here: 27.7 us
  starting transfers between devices  10.9 us (39%)
  Pallas kernels  10.5 us (38%)
  between operations  3.31 us (12%)
  waiting for transfers between devices  2.9 us (10%)
    ppermute x3, starting transfers between devices, on_device(): columns[shift] = lax.ppermute(column, 'tile', ring)  5.57 us
    pallas_call x1, Pallas kernels, pair_sums(): pl.pallas_call(functools.partial(early_kernel, early, rim), out_shape=(re...  3.73 us
    pallas_call x1, Pallas kernels, pair_sums(): pl.pallas_call(functools.partial(other_kernel, arrivals, early, rim), out...  3.23 us
    ppermute x1, starting transfers between devices, on_device(): partner = lax.ppermute(pair, 'tile', across)  3 us
    pallas_call x1, Pallas kernels, own(): pl.pallas_call(own_kernel, out_shape=partial, in_specs=[VMEM] * 6, out_sp...  1.8 us
    ppermute x1, waiting for transfers between devices, on_device(): other = lax.ppermute(other, 'tile', across)  1.49 us
    ppermute x1, waiting for transfers between devices, on_device(): far = lax.ppermute(far, 'slab', odds)  1.4 us
    ppermute x1, starting transfers between devices, on_device(): near = lax.ppermute(near, 'slab', evens)  0.96 us
  transfers between devices with their start and end apart: 7, of which 2 were waited for; matrix products, arithmetic and copies ran while one was open for 0% of the time, Pallas kernels for 20%

profile of v3, /device:TPU:0, one launch (start us, length us, event | category | flops | bytes accessed | tf_op | source)
XLA Modules:
  0.0 27.7 jit_solution(5482929981163729415)
XLA Ops:
  0.6 0.9 %pack.1.pair = f32[8,2176]{1,0:T(8,128)S(1)} custom-call(f32[8,2048]{1,0:T(8,128)} %particles.3, s32[1,128]{1,0:T(1,128)} %first.1, s32[1,128]{1,0:T(1,128)} %second.1, s32[1,128]{1,0:T(1,128)} %live.1), custom_call_target="tpu_custom_call" | custom-call | tf_op jit(solution)/shard_map/pack/pallas_call | solution.py:435
  1.6 3.0 %collective-permute-start = (f32[8,2176]{1,0:T(8,128)S(1)}, f32[8,2176]{1,0:T(8,128)S(1)}, u32[]{:S(2)}, u32[]{:S(2)}) collective-permute-start(f32[8,2176]{1,0:T(8,128)S(1)} %pack.1.pair), channel_id=1, source_target_pairs={{0,1},{1,0},{2,3},{3,2},{4,5},{5,4},{6,7},{7,6},{8,9},{9,8},{10,11... | collective-permute-start | bytes 208904 | tf_op jit(solution)/shard_map/ppermute | solution.py:450
  5.9 0.7 %collective-permute-start.1 = (f32[8,128]{1,0:T(8,128)S(1)}, f32[8,128]{1,0:T(8,128)S(1)}, u32[]{:S(2)}, u32[]{:S(2)}) collective-permute-start(f32[8,128]{1,0:T(8,128)S(1)} %get-tuple-element.10), channel_id=1, source_target_pairs={{0,24},{8,16},{16,8},{24,0},{1,25},{9,17},{17,9},{25,1},{2,26},{10... | collective-permute-start | bytes 12296 | tf_op jit(solution)/shard_map/ppermute | solution.py:459
  6.6 1.0 %collective-permute-start.2 = (f32[8,128]{1,0:T(8,128)S(1)}, f32[8,128]{1,0:T(8,128)S(1)}, u32[]{:S(2)}, u32[]{:S(2)}) collective-permute-start(f32[8,128]{1,0:T(8,128)S(1)} %get-tuple-element.11), channel_id=1, source_target_pairs={{0,8},{8,0},{16,24},{24,16},{1,9},{9,1},{17,25},{25,17},{2,10},{10... | collective-permute-start | bytes 12296 | tf_op jit(solution)/shard_map/ppermute | solution.py:460
  7.6 1.4 %collective-permute-done.1.far = f32[8,128]{1,0:T(8,128)S(1)} collective-permute-done((f32[8,128]{1,0:T(8,128)S(1)}, f32[8,128]{1,0:T(8,128)S(1)}, u32[]{:S(2)}, u32[]{:S(2)}) %collective-permute-start.1) | collective-permute-done | bytes 4128 | tf_op jit(solution)/shard_map/ppermute | solution.py:459
  9.0 0.0 collective-permute-done.2.near
  9.0 0.0 collective-permute-done.partner.refs_2_.refs_4_
  9.0 1.6 %collective-permute-start.3 = (f32[8,2432]{1,0:T(8,128)S(1)}, f32[8,2432]{1,0:T(8,128)S(1)}, u32[]{:S(2)}, u32[]{:S(2)}) collective-permute-start(f32[8,2432]{1,0:T(8,128)S(1)} %join.1.refs_0_.column), channel_id=1, source_target_pairs={{0,2},{1,3},{2,4},{3,5},{4,6},{5,7},{6,0},{7,1},{8,10},{9,11},{10,... | collective-permute-start | bytes 233480 | tf_op jit(solution)/shard_map/ppermute | solution.py:473
  10.6 2.6 %collective-permute-start.4 = (f32[8,2432]{1,0:T(8,128)S(1)}, f32[8,2432]{1,0:T(8,128)S(1)}, u32[]{:S(2)}, u32[]{:S(2)}) collective-permute-start(f32[8,2432]{1,0:T(8,128)S(1)} %join.1.refs_0_.column), channel_id=1, source_target_pairs={{0,4},{1,5},{2,6},{3,7},{4,0},{5,1},{6,2},{7,3},{8,12},{9,13},{10,... | collective-permute-start | bytes 233480 | tf_op jit(solution)/shard_map/ppermute | solution.py:473
  13.2 1.3 %collective-permute-start.5 = (f32[8,2432]{1,0:T(8,128)S(1)}, f32[8,2432]{1,0:T(8,128)S(1)}, u32[]{:S(2)}, u32[]{:S(2)}) collective-permute-start(f32[8,2432]{1,0:T(8,128)S(1)} %join.1.refs_0_.column), channel_id=1, source_target_pairs={{0,6},{1,7},{2,0},{3,1},{4,2},{5,3},{6,4},{7,5},{8,14},{9,15},{10,... | collective-permute-start | bytes 233480 | tf_op jit(solution)/shard_map/ppermute | solution.py:473
  15.9 0.0 collective-permute-done.3.refs_1_
  15.9 3.7 %pairs_early.1 = (bf16[33,128,512]{2,1,0:T(8,128)(2,1)S(1)}, f32[33,16,128]{2,1,0:T(8,128)S(1)}) custom-call(f32[8,2432]{1,0:T(8,128)S(1)} %join.1.refs_0_.column, f32[8,2432]{1,0:T(8,128)S(1)} %collective-permute-done.3.refs_1_, f32[8,2176]{1,0:T(8,128)S(1)} %collective-permute-done.partner.refs_2_.refs_4_), custom_call_target="tpu_custom_call" | custom-call | flops 8000000 | bytes 8000000 | tf_op jit(solution)/shard_map/pairs_early/pallas_call | solution.py:379
  19.6 0.0 collective-permute-done.4.refs_2_
  19.6 0.0 collective-permute-done.5.refs_3_
  19.7 3.2 %pairs_other.1 = (f32[4,2048]{1,0:T(4,128)S(1)}, s32[8,128]{1,0:T(8,128)S(1)}, bf16[72,128,128]{2,1,0:T(8,128)(2,1)S(1)}, bf16[72,32,256]{2,1,0:T(8,128)(2,1)S(1)}) custom-call(f32[8,2432]{1,0:T(8,128)S(1)} %join.1.refs_0_.column, f32[8,2432]{1,0:T(8,128)S(1)} %collective-permute-done.3.refs_1_, f32[8,2432]{1,0:T(8,128)S(1)} %collective-permute-done.4.refs_2_, ...), custom_call_target="tpu_custom_call" | custom-call | tf_op jit(solution)/shard_map/pairs_other/pallas_call | solution.py:397
  22.9 0.6 %collective-permute-start.6 = (f32[4,2048]{1,0:T(4,128)S(1)}, f32[4,2048]{1,0:T(4,128)S(1)}, u32[]{:S(2)}, u32[]{:S(2)}) collective-permute-start(f32[4,2048]{1,0:T(4,128)S(1)} %get-tuple-element.17), channel_id=1, source_target_pairs={{0,1},{1,0},{2,3},{3,2},{4,5},{5,4},{6,7},{7,6},{8,9},{9,8},{10,11... | collective-permute-start | bytes 98312 | tf_op jit(solution)/shard_map/ppermute | solution.py:477
  23.5 0.1 pad_maximum_fusion
  23.6 0.0 copy-start
  23.6 1.8 %pairs_own.1.own = f32[4,2048]{1,0:T(4,128)S(1)} custom-call(s32[8,128]{1,0:T(8,128)S(1)} %get-tuple-element.14.codes, bf16[72,128,128]{2,1,0:T(8,128)(2,1)S(1)} %get-tuple-element.15.acting, bf16[72,32,256]{2,1,0:T(8,128)(2,1)S(1)} %get-tuple-element.16.summing, bf16[33,128,512]{2,1,0:T(8,128)(2,1)S(1)} %get-tuple-element.12.refs_5_.receiving, ...), custom_call_target="tpu_custom_call" | custom-call | tf_op jit(solution)/shard_map/pairs_own/pallas_call | solution.py:412
  25.4 1.5 %collective-permute-done.6.other = f32[4,2048]{1,0:T(4,128)S(1)} collective-permute-done((f32[4,2048]{1,0:T(4,128)S(1)}, f32[4,2048]{1,0:T(4,128)S(1)}, u32[]{:S(2)}, u32[]{:S(2)}) %collective-permute-start.6) | collective-permute-done | bytes 32800 | tf_op jit(solution)/shard_map/ppermute | solution.py:477
  26.9 0.1 broadcast_in_dim.2.step
  26.9 0.0 copy-done
  26.9 0.7 %advance.1 = (f32[4,2048]{1,0:T(4,128)}, f32[7,2048]{1,0:T(8,128)}) custom-call(f32[2,128]{1,0:T(2,128)S(1)} %broadcast_in_dim.2.step, f32[8,2048]{1,0:T(8,128)S(1)} %copy-done, f32[4,2048]{1,0:T(4,128)S(1)} %pairs_own.1.own, f32[4,2048]{1,0:T(4,128)S(1)} %collective-permute-done.6.other), custom_call_target="tpu_custom_call" | custom-call | tf_op jit(solution)/shard_map/advance/pallas_call | solution.py:478
  (2 shorter events, 0.0 us)
Async XLA Ops:
  1.6 7.4 %collective-permute-start = (f32[8,2176]{1,0:T(8,128)S(1)}, f32[8,2176]{1,0:T(8,128)S(1)}, u32[]{:S(2)}, u32[]{:S(2)}) collective-permute-start(f32[8,2176]{1,0:T(8,128)S(1)} %pack.1.pair), channel_id=1, source_target_pairs={{0,1},{1,0},{2,3},{3,2},{4,5},{5,4},{6,7},{7,6},{8,9},{9,8},{10,11... | collective-permute-start | bytes 208904 | tf_op jit(solution)/shard_map/ppermute | solution.py:450
  5.9 3.1 %collective-permute-start.1 = (f32[8,128]{1,0:T(8,128)S(1)}, f32[8,128]{1,0:T(8,128)S(1)}, u32[]{:S(2)}, u32[]{:S(2)}) collective-permute-start(f32[8,128]{1,0:T(8,128)S(1)} %get-tuple-element.10), channel_id=1, source_target_pairs={{0,24},{8,16},{16,8},{24,0},{1,25},{9,17},{17,9},{25,1},{2,26},{10... | collective-permute-start | bytes 12296 | tf_op jit(solution)/shard_map/ppermute | solution.py:459
  6.6 2.4 %collective-permute-start.2 = (f32[8,128]{1,0:T(8,128)S(1)}, f32[8,128]{1,0:T(8,128)S(1)}, u32[]{:S(2)}, u32[]{:S(2)}) collective-permute-start(f32[8,128]{1,0:T(8,128)S(1)} %get-tuple-element.11), channel_id=1, source_target_pairs={{0,8},{8,0},{16,24},{24,16},{1,9},{9,1},{17,25},{25,17},{2,10},{10... | collective-permute-start | bytes 12296 | tf_op jit(solution)/shard_map/ppermute | solution.py:460
  9.0 6.9 %collective-permute-start.3 = (f32[8,2432]{1,0:T(8,128)S(1)}, f32[8,2432]{1,0:T(8,128)S(1)}, u32[]{:S(2)}, u32[]{:S(2)}) collective-permute-start(f32[8,2432]{1,0:T(8,128)S(1)} %join.1.refs_0_.column), channel_id=1, source_target_pairs={{0,2},{1,3},{2,4},{3,5},{4,6},{5,7},{6,0},{7,1},{8,10},{9,11},{10,... | collective-permute-start | bytes 233480 | tf_op jit(solution)/shard_map/ppermute | solution.py:473
  10.6 9.0 %collective-permute-start.4 = (f32[8,2432]{1,0:T(8,128)S(1)}, f32[8,2432]{1,0:T(8,128)S(1)}, u32[]{:S(2)}, u32[]{:S(2)}) collective-permute-start(f32[8,2432]{1,0:T(8,128)S(1)} %join.1.refs_0_.column), channel_id=1, source_target_pairs={{0,4},{1,5},{2,6},{3,7},{4,0},{5,1},{6,2},{7,3},{8,12},{9,13},{10,... | collective-permute-start | bytes 233480 | tf_op jit(solution)/shard_map/ppermute | solution.py:473
  13.2 6.4 %collective-permute-start.5 = (f32[8,2432]{1,0:T(8,128)S(1)}, f32[8,2432]{1,0:T(8,128)S(1)}, u32[]{:S(2)}, u32[]{:S(2)}) collective-permute-start(f32[8,2432]{1,0:T(8,128)S(1)} %join.1.refs_0_.column), channel_id=1, source_target_pairs={{0,6},{1,7},{2,0},{3,1},{4,2},{5,3},{6,4},{7,5},{8,14},{9,15},{10,... | collective-permute-start | bytes 233480 | tf_op jit(solution)/shard_map/ppermute | solution.py:473
  22.9 4.0 %collective-permute-start.6 = (f32[4,2048]{1,0:T(4,128)S(1)}, f32[4,2048]{1,0:T(4,128)S(1)}, u32[]{:S(2)}, u32[]{:S(2)}) collective-permute-start(f32[4,2048]{1,0:T(4,128)S(1)} %get-tuple-element.17), channel_id=1, source_target_pairs={{0,1},{1,0},{2,3},{3,2},{4,5},{5,4},{6,7},{7,6},{8,9},{9,8},{10,11... | collective-permute-start | bytes 98312 | tf_op jit(solution)/shard_map/ppermute | solution.py:477
  23.6 3.4 %copy-start = (f32[8,2048]{1,0:T(8,128)S(1)}, f32[8,2048]{1,0:T(8,128)}, u32[]{:S(2)}) copy-start(f32[8,2048]{1,0:T(8,128)} %particles.3) | copy-start | bytes 196612

commit v4 on v3

--- a/solution.py
+++ b/solution.py
@@ -23,7 +23,7 @@
 SCALE_SQ = SCALE * SCALE
 CENTRE = 1.5
 DENSITY_SCALE = -0.5 / (VISCOSITY * SOUND_SPEED * SMOOTHING * SCALE_SQ)
-BATCH = 16
+BATCH = 32
 ROWS = 32
 
 F32 = jnp.float32
@@ -133,17 +133,25 @@
             sums[targets[lot], 0:8, :] += closings[lot]
             sums[targets[lot], 8:16, :] += total[0:8] + total[8:16] + total[16:24]
 
+    quarter = BATCH // 4
+    turns = lax.div(count + quarter - 1, BATCH)
+
     def full(turn, carry):
         work(turn * BATCH, BATCH)
         return carry
 
-    half = BATCH // 2
-    turns = lax.div(count + half - 1, BATCH)
     lax.fori_loop(0, turns, full, 0)
-
-    @pl.when(count > turns * BATCH)
+    done = turns * BATCH
+
+    @pl.when(count > done + quarter)
     def _():
-        work(turns * BATCH, half)
+        work(done, 2 * quarter)
+
+    done = done + jnp.where(count > done + quarter, 2 * quarter, 0)
+
+    @pl.when(count > done)
+    def _():
+        work(done, quarter)
 
 
 def write_rates(sums, base, source, out):

time: 27.9 us -> 27.4 us (0.982)
  Pallas kernels: 10.5 us -> 9.82 us
    pallas_call x1, Pallas kernels: 3.73 us -> 2.21 us  [pair_sums(): pl.pallas_call(functools.partial(early_kernel, early, rim), out_shape=(re...]
    ppermute x3, waiting for transfers between devices: 0.01 us -> 0.86 us  [on_device(): columns[shift] = lax.ppermute(column, 'tile', ring)]
    ppermute x1, waiting for transfers between devices: 1.49 us -> 0.74 us  [on_device(): other = lax.ppermute(other, 'tile', across)]
    pallas_call x1, Pallas kernels: 1.8 us -> 2.54 us  [own(): pl.pallas_call(own_kernel, out_shape=partial, in_specs=[VMEM] * 6, out_sp...]
  transfers between devices with their start and end apart: 7 -> 7, of which waited for: 2 -> 4; matrix products, arithmetic and copies ran while one was open for 0% -> 0% of each run, Pallas kernels for 20% -> 18%
where the time goes in v4:
time: 27.4 us; the launch traced here: 27.2 us
  starting transfers between devices  10.9 us (40%)
  Pallas kernels  9.82 us (36%)
  between operations  3.29 us (12%)
  waiting for transfers between devices  3.01 us (11%)
    ppermute x3, starting transfers between devices, on_device(): columns[shift] = lax.ppermute(column, 'tile', ring)  5.57 us
    pallas_call x1, Pallas kernels, pair_sums(): pl.pallas_call(functools.partial(other_kernel, arrivals, early, rim), out...  3.38 us
    ppermute x1, starting transfers between devices, on_device(): partner = lax.ppermute(pair, 'tile', across)  3 us
    pallas_call x1, Pallas kernels, own(): pl.pallas_call(own_kernel, out_shape=partial, in_specs=[VMEM] * 6, out_sp...  2.54 us
    pallas_call x1, Pallas kernels, pair_sums(): pl.pallas_call(functools.partial(early_kernel, early, rim), out_shape=(re...  2.21 us
    ppermute x1, waiting for transfers between devices, on_device(): far = lax.ppermute(far, 'slab', odds)  1.4 us
    ppermute x1, starting transfers between devices, on_device(): near = lax.ppermute(near, 'slab', evens)  0.96 us
    pallas_call x1, Pallas kernels, on_device(): pl.pallas_call(pack_kernel, out_shape=jax.ShapeDtypeStruct((8, width + PB...  0.93 us
  transfers between devices with their start and end apart: 7, of which 4 were waited for; matrix products, arithmetic and copies ran while one was open for 0% of the time, Pallas kernels for 18%

profile of v4, /device:TPU:0, one launch (start us, length us, event | category | flops | bytes accessed | tf_op | source)
XLA Modules:
  0.0 27.2 jit_solution(4919491523188495311)
XLA Ops:
  0.6 0.9 %pack.1.pair = f32[8,2176]{1,0:T(8,128)S(1)} custom-call(f32[8,2048]{1,0:T(8,128)} %particles.3, s32[1,128]{1,0:T(1,128)} %first.1, s32[1,128]{1,0:T(1,128)} %second.1, s32[1,128]{1,0:T(1,128)} %live.1), custom_call_target="tpu_custom_call" | custom-call | tf_op jit(solution)/shard_map/pack/pallas_call | solution.py:443
  1.6 3.0 %collective-permute-start = (f32[8,2176]{1,0:T(8,128)S(1)}, f32[8,2176]{1,0:T(8,128)S(1)}, u32[]{:S(2)}, u32[]{:S(2)}) collective-permute-start(f32[8,2176]{1,0:T(8,128)S(1)} %pack.1.pair), channel_id=1, source_target_pairs={{0,1},{1,0},{2,3},{3,2},{4,5},{5,4},{6,7},{7,6},{8,9},{9,8},{10,11... | collective-permute-start | bytes 208904 | tf_op jit(solution)/shard_map/ppermute | solution.py:458
  5.9 0.7 %collective-permute-start.1 = (f32[8,128]{1,0:T(8,128)S(1)}, f32[8,128]{1,0:T(8,128)S(1)}, u32[]{:S(2)}, u32[]{:S(2)}) collective-permute-start(f32[8,128]{1,0:T(8,128)S(1)} %get-tuple-element.10), channel_id=1, source_target_pairs={{0,24},{8,16},{16,8},{24,0},{1,25},{9,17},{17,9},{25,1},{2,26},{10... | collective-permute-start | bytes 12296 | tf_op jit(solution)/shard_map/ppermute | solution.py:467
  6.6 1.0 %collective-permute-start.2 = (f32[8,128]{1,0:T(8,128)S(1)}, f32[8,128]{1,0:T(8,128)S(1)}, u32[]{:S(2)}, u32[]{:S(2)}) collective-permute-start(f32[8,128]{1,0:T(8,128)S(1)} %get-tuple-element.11), channel_id=1, source_target_pairs={{0,8},{8,0},{16,24},{24,16},{1,9},{9,1},{17,25},{25,17},{2,10},{10... | collective-permute-start | bytes 12296 | tf_op jit(solution)/shard_map/ppermute | solution.py:468
  7.6 1.4 %collective-permute-done.1.far = f32[8,128]{1,0:T(8,128)S(1)} collective-permute-done((f32[8,128]{1,0:T(8,128)S(1)}, f32[8,128]{1,0:T(8,128)S(1)}, u32[]{:S(2)}, u32[]{:S(2)}) %collective-permute-start.1) | collective-permute-done | bytes 4128 | tf_op jit(solution)/shard_map/ppermute | solution.py:467
  9.0 0.0 collective-permute-done.2.near
  9.0 0.0 collective-permute-done.partner.refs_2_.refs_4_
  9.0 1.6 %collective-permute-start.3 = (f32[8,2432]{1,0:T(8,128)S(1)}, f32[8,2432]{1,0:T(8,128)S(1)}, u32[]{:S(2)}, u32[]{:S(2)}) collective-permute-start(f32[8,2432]{1,0:T(8,128)S(1)} %join.1.refs_0_.column), channel_id=1, source_target_pairs={{0,2},{1,3},{2,4},{3,5},{4,6},{5,7},{6,0},{7,1},{8,10},{9,11},{10,... | collective-permute-start | bytes 233480 | tf_op jit(solution)/shard_map/ppermute | solution.py:481
  10.6 2.6 %collective-permute-start.4 = (f32[8,2432]{1,0:T(8,128)S(1)}, f32[8,2432]{1,0:T(8,128)S(1)}, u32[]{:S(2)}, u32[]{:S(2)}) collective-permute-start(f32[8,2432]{1,0:T(8,128)S(1)} %join.1.refs_0_.column), channel_id=1, source_target_pairs={{0,4},{1,5},{2,6},{3,7},{4,0},{5,1},{6,2},{7,3},{8,12},{9,13},{10,... | collective-permute-start | bytes 233480 | tf_op jit(solution)/shard_map/ppermute | solution.py:481
  13.2 1.3 %collective-permute-start.5 = (f32[8,2432]{1,0:T(8,128)S(1)}, f32[8,2432]{1,0:T(8,128)S(1)}, u32[]{:S(2)}, u32[]{:S(2)}) collective-permute-start(f32[8,2432]{1,0:T(8,128)S(1)} %join.1.refs_0_.column), channel_id=1, source_target_pairs={{0,6},{1,7},{2,0},{3,1},{4,2},{5,3},{6,4},{7,5},{8,14},{9,15},{10,... | collective-permute-start | bytes 233480 | tf_op jit(solution)/shard_map/ppermute | solution.py:481
  15.9 0.0 collective-permute-done.3.refs_1_
  15.9 2.2 %pairs_early.1 = (bf16[33,128,512]{2,1,0:T(8,128)(2,1)S(1)}, f32[33,16,128]{2,1,0:T(8,128)S(1)}) custom-call(f32[8,2432]{1,0:T(8,128)S(1)} %join.1.refs_0_.column, f32[8,2432]{1,0:T(8,128)S(1)} %collective-permute-done.3.refs_1_, f32[8,2176]{1,0:T(8,128)S(1)} %collective-permute-done.partner.refs_2_.refs_4_), custom_call_target="tpu_custom_call" | custom-call | flops 8000000 | bytes 8000000 | tf_op jit(solution)/shard_map/pairs_early/pallas_call | solution.py:387
  18.1 0.6 %collective-permute-done.4.refs_2_ = f32[8,2432]{1,0:T(8,128)S(1)} collective-permute-done((f32[8,2432]{1,0:T(8,128)S(1)}, f32[8,2432]{1,0:T(8,128)S(1)}, u32[]{:S(2)}, u32[]{:S(2)}) %collective-permute-start.4) | collective-permute-done | bytes 77856 | tf_op jit(solution)/shard_map/ppermute | solution.py:481
  18.8 0.2 collective-permute-done.5.refs_3_
  19.0 3.4 %pairs_other.1 = (f32[4,2048]{1,0:T(4,128)S(1)}, s32[8,128]{1,0:T(8,128)S(1)}, bf16[72,128,128]{2,1,0:T(8,128)(2,1)S(1)}, bf16[72,32,256]{2,1,0:T(8,128)(2,1)S(1)}) custom-call(f32[8,2432]{1,0:T(8,128)S(1)} %join.1.refs_0_.column, f32[8,2432]{1,0:T(8,128)S(1)} %collective-permute-done.3.refs_1_, f32[8,2432]{1,0:T(8,128)S(1)} %collective-permute-done.4.refs_2_, ...), custom_call_target="tpu_custom_call" | custom-call | tf_op jit(solution)/shard_map/pairs_other/pallas_call | solution.py:405
  22.4 0.6 %collective-permute-start.6 = (f32[4,2048]{1,0:T(4,128)S(1)}, f32[4,2048]{1,0:T(4,128)S(1)}, u32[]{:S(2)}, u32[]{:S(2)}) collective-permute-start(f32[4,2048]{1,0:T(4,128)S(1)} %get-tuple-element.17), channel_id=1, source_target_pairs={{0,1},{1,0},{2,3},{3,2},{4,5},{5,4},{6,7},{7,6},{8,9},{9,8},{10,11... | collective-permute-start | bytes 98312 | tf_op jit(solution)/shard_map/ppermute | solution.py:485
  23.0 0.1 pad_maximum_fusion
  23.1 0.0 copy-start
  23.1 2.5 %pairs_own.1.own = f32[4,2048]{1,0:T(4,128)S(1)} custom-call(s32[8,128]{1,0:T(8,128)S(1)} %get-tuple-element.14.codes, bf16[72,128,128]{2,1,0:T(8,128)(2,1)S(1)} %get-tuple-element.15.acting, bf16[72,32,256]{2,1,0:T(8,128)(2,1)S(1)} %get-tuple-element.16.summing, bf16[33,128,512]{2,1,0:T(8,128)(2,1)S(1)} %get-tuple-element.12.refs_5_.receiving, ...), custom_call_target="tpu_custom_call" | custom-call | tf_op jit(solution)/shard_map/pairs_own/pallas_call | solution.py:420
  25.6 0.7 %collective-permute-done.6.other = f32[4,2048]{1,0:T(4,128)S(1)} collective-permute-done((f32[4,2048]{1,0:T(4,128)S(1)}, f32[4,2048]{1,0:T(4,128)S(1)}, u32[]{:S(2)}, u32[]{:S(2)}) %collective-permute-start.6) | collective-permute-done | bytes 32800 | tf_op jit(solution)/shard_map/ppermute | solution.py:485
  26.3 0.1 broadcast_in_dim.2.step
  26.4 0.0 copy-done
  26.4 0.7 %advance.1 = (f32[4,2048]{1,0:T(4,128)}, f32[7,2048]{1,0:T(8,128)}) custom-call(f32[2,128]{1,0:T(2,128)S(1)} %broadcast_in_dim.2.step, f32[8,2048]{1,0:T(8,128)S(1)} %copy-done, f32[4,2048]{1,0:T(4,128)S(1)} %pairs_own.1.own, f32[4,2048]{1,0:T(4,128)S(1)} %collective-permute-done.6.other), custom_call_target="tpu_custom_call" | custom-call | tf_op jit(solution)/shard_map/advance/pallas_call | solution.py:486
  (2 shorter events, 0.0 us)
Async XLA Ops:
  1.6 7.4 %collective-permute-start = (f32[8,2176]{1,0:T(8,128)S(1)}, f32[8,2176]{1,0:T(8,128)S(1)}, u32[]{:S(2)}, u32[]{:S(2)}) collective-permute-start(f32[8,2176]{1,0:T(8,128)S(1)} %pack.1.pair), channel_id=1, source_target_pairs={{0,1},{1,0},{2,3},{3,2},{4,5},{5,4},{6,7},{7,6},{8,9},{9,8},{10,11... | collective-permute-start | bytes 208904 | tf_op jit(solution)/shard_map/ppermute | solution.py:458
  5.9 3.1 %collective-permute-start.1 = (f32[8,128]{1,0:T(8,128)S(1)}, f32[8,128]{1,0:T(8,128)S(1)}, u32[]{:S(2)}, u32[]{:S(2)}) collective-permute-start(f32[8,128]{1,0:T(8,128)S(1)} %get-tuple-element.10), channel_id=1, source_target_pairs={{0,24},{8,16},{16,8},{24,0},{1,25},{9,17},{17,9},{25,1},{2,26},{10... | collective-permute-start | bytes 12296 | tf_op jit(solution)/shard_map/ppermute | solution.py:467
  6.6 2.4 %collective-permute-start.2 = (f32[8,128]{1,0:T(8,128)S(1)}, f32[8,128]{1,0:T(8,128)S(1)}, u32[]{:S(2)}, u32[]{:S(2)}) collective-permute-start(f32[8,128]{1,0:T(8,128)S(1)} %get-tuple-element.11), channel_id=1, source_target_pairs={{0,8},{8,0},{16,24},{24,16},{1,9},{9,1},{17,25},{25,17},{2,10},{10... | collective-permute-start | bytes 12296 | tf_op jit(solution)/shard_map/ppermute | solution.py:468
  9.0 6.9 %collective-permute-start.3 = (f32[8,2432]{1,0:T(8,128)S(1)}, f32[8,2432]{1,0:T(8,128)S(1)}, u32[]{:S(2)}, u32[]{:S(2)}) collective-permute-start(f32[8,2432]{1,0:T(8,128)S(1)} %join.1.refs_0_.column), channel_id=1, source_target_pairs={{0,2},{1,3},{2,4},{3,5},{4,6},{5,7},{6,0},{7,1},{8,10},{9,11},{10,... | collective-permute-start | bytes 233480 | tf_op jit(solution)/shard_map/ppermute | solution.py:481
  10.6 8.1 %collective-permute-start.4 = (f32[8,2432]{1,0:T(8,128)S(1)}, f32[8,2432]{1,0:T(8,128)S(1)}, u32[]{:S(2)}, u32[]{:S(2)}) collective-permute-start(f32[8,2432]{1,0:T(8,128)S(1)} %join.1.refs_0_.column), channel_id=1, source_target_pairs={{0,4},{1,5},{2,6},{3,7},{4,0},{5,1},{6,2},{7,3},{8,12},{9,13},{10,... | collective-permute-start | bytes 233480 | tf_op jit(solution)/shard_map/ppermute | solution.py:481
  13.2 5.7 %collective-permute-start.5 = (f32[8,2432]{1,0:T(8,128)S(1)}, f32[8,2432]{1,0:T(8,128)S(1)}, u32[]{:S(2)}, u32[]{:S(2)}) collective-permute-start(f32[8,2432]{1,0:T(8,128)S(1)} %join.1.refs_0_.column), channel_id=1, source_target_pairs={{0,6},{1,7},{2,0},{3,1},{4,2},{5,3},{6,4},{7,5},{8,14},{9,15},{10,... | collective-permute-start | bytes 233480 | tf_op jit(solution)/shard_map/ppermute | solution.py:481
  22.4 4.0 %collective-permute-start.6 = (f32[4,2048]{1,0:T(4,128)S(1)}, f32[4,2048]{1,0:T(4,128)S(1)}, u32[]{:S(2)}, u32[]{:S(2)}) collective-permute-start(f32[4,2048]{1,0:T(4,128)S(1)} %get-tuple-element.17), channel_id=1, source_target_pairs={{0,1},{1,0},{2,3},{3,2},{4,5},{5,4},{6,7},{7,6},{8,9},{9,8},{10,11... | collective-permute-start | bytes 98312 | tf_op jit(solution)/shard_map/ppermute | solution.py:485
  23.1 3.4 %copy-start = (f32[8,2048]{1,0:T(8,128)S(1)}, f32[8,2048]{1,0:T(8,128)}, u32[]{:S(2)}) copy-start(f32[8,2048]{1,0:T(8,128)} %particles.3) | copy-start | bytes 196612
